TPU v7x, 128 devices: a whole 4x4x4 slice. The times are simulated.
128 devices in a mesh: dev: 128 (over y, x, z, core).
Axes of the slice: x: 4, y: 4, z: 4, core: 2. Of those that a mesh axis runs over, the one named last changes fastest.
Arguments:
- features: bfloat16 [32768, 128], P('dev'), may hold values from -6 to 6
- weight: bfloat16 [128, 256], replicated, may hold values from -0.5 to 0.5
- tile_values: bfloat16 [256, 32, 128, 128], P('dev'), may hold values from -0.09375 to 0.09375
- tile_cols: int32 [256, 32], P('dev'), may hold values from 0 to 255, as said below
- tile_counts: int32 [256, 32], P('dev'), may hold values from 0 to 16384, as said below
- cotangent: bfloat16 [32768, 256], P('dev'), may hold values from -6 to 6
Outputs:
- activations: bfloat16 [32768, 256], P('dev')
- features_grad: float32 [32768, 128], P('dev')
- weight_grad: float32 [128, 256], P('dev')
Inputs may be any that keep to these rules, and one draw needn't show every extreme that they name: `tile_cols`: within a row block the column blocks of the slots are distinct. `tile_counts`: A slot is live where its count is above 0; the live slots of a row block come first, every row block has at least half of its 32 slots live (and at least one), and some row block has all live.
All inputs are finite; a program needn't handle non-finite values.
Results may differ from a plain program's by a relative error of at most 0.0061.
Values may be sent and summed in bfloat16 or wider, within the bound.
A program may use at most 128 MiB of HBM per device.

v0:
```python
import jax
import jax.numpy as jnp
from jax import lax
from jax.sharding import PartitionSpec as P


def on_device(features, weight, tile_values, tile_cols, tile_counts, cotangent):
    device_count = lax.axis_size("dev")
    own_index = lax.axis_index("dev")
    row_count, in_width = features.shape
    block_count, slot_count, tile_size, _ = tile_values.shape
    live = (tile_counts > 0).astype(jnp.float32)
    gathered = lax.all_gather(features, "dev", axis=0, tiled=True)
    feature_blocks = gathered.reshape(-1, tile_size, in_width)
    picked = feature_blocks[tile_cols.reshape(-1)].reshape(
        block_count, slot_count, tile_size, in_width
    )
    products = jnp.einsum(
        "bsij,bsjf->bsif", tile_values, picked, preferred_element_type=jnp.float32
    )
    summed = jnp.sum(products * live[:, :, None, None], axis=1)
    aggregated = summed.reshape(row_count, in_width).astype(jnp.bfloat16)
    pre = jnp.dot(aggregated, weight, preferred_element_type=jnp.float32)
    activations = jax.nn.silu(pre).astype(jnp.bfloat16)
    sigma = jax.nn.sigmoid(pre)
    delta = (cotangent.astype(jnp.float32) * sigma * (1.0 + pre * (1.0 - sigma))).astype(
        jnp.bfloat16
    )
    back = lax.dot_general(
        delta, weight, (((1,), (1,)), ((), ())), preferred_element_type=jnp.float32
    ).astype(jnp.bfloat16)
    back_blocks = back.reshape(block_count, tile_size, in_width)
    terms = jnp.einsum(
        "bsij,bif->bsjf", tile_values, back_blocks, preferred_element_type=jnp.float32
    )
    tile_terms = (terms * live[:, :, None, None]).astype(jnp.bfloat16)
    widened = lax.optimization_barrier(tile_terms).astype(jnp.float32)
    scattered = jax.ops.segment_sum(
        widened.reshape(-1, tile_size, in_width),
        tile_cols.reshape(-1),
        num_segments=device_count * block_count,
    )
    column_terms = scattered.reshape(device_count * row_count, in_width)
    features_grad = lax.psum_scatter(column_terms, "dev", scatter_dimension=0, tiled=True)
    local_weight = lax.dot_general(
        aggregated, delta, (((0,), (0,)), ((), ())), preferred_element_type=jnp.float32
    )
    share_rows = in_width // device_count
    weight_total = lax.psum(local_weight, "dev")
    weight_grad = lax.dynamic_slice_in_dim(weight_total, own_index * share_rows, share_rows, 0)
    return (activations, features_grad, weight_grad)


def solution(mesh):
    return jax.shard_map(
        on_device,
        mesh=mesh,
        in_specs=(
            P("dev", None),
            P(),
            P("dev", None, None, None),
            P("dev", None),
            P("dev", None),
            P("dev", None),
        ),
        out_specs=(P("dev", None), P("dev", None), P("dev", None)),
        check_vma=False,
    )
```

profile of v0, /device:TPU:0, one launch (start us, length us, event | category | flops | bytes accessed | tf_op | source)
XLA Modules:
  0.0 906.4 jit_solution(7230514647587300065)
XLA Ops:
  7.2 0.0 copy-start
  7.2 0.0 all-gather.2.cloned.1.call-start
  7.2 0.7 all-gather.2.cloned.1.call-update
  7.9 0.0 all-reduce.2.cloned.1.call-start
  8.0 0.8 reshape.77
  8.7 0.8 reshape.59
  9.5 0.7 compare_convert_fusion
  10.2 73.4 %all-gather.2.cloned.1.call-done = bf16[32768,128]{1,0:T(8,128)(2,1)} async-done(((bf16[256,128]{1,0:T(8,128)(2,1)}), bf16[32768,128]{1,0:T(8,128)(2,1)}) %all-gather.2.cloned.1.call-update) | async-done | bytes 8388624 | tf_op jit(solution)/shard_map/all_gather | solution.py:13
  83.6 0.0 copy-start.1
  83.6 0.0 copy-start.2
  83.6 5.6 gather_fusion
  89.2 0.0 copy-done
  89.2 3.2 multiply_reduce_fusion
  92.4 0.1 copy.15
  92.6 0.0 copy-done.1
  92.6 0.0 copy-done.2
  92.6 0.9 multiply_convert_fusion.1
  93.5 0.8 fusion.2
  94.3 0.2 convolution_convert_fusion
  94.5 0.0 all-reduce.2.cloned.1.call-update
  94.6 0.0 reduce-scatter.2.cloned.1.call-start
  94.6 0.8 fusion
  95.4 2.6 bitcast_convert_fusion
  98.0 5.6 copy.17
  103.6 7.9 broadcast_in_dim.2
  111.4 13.7 %scatter_fusion = f32[256,128,128]{2,1,0:T(8,128)} fusion(f32[256,128,128]{2,1,0:T(8,128)} %broadcast_in_dim.2, s32[64]{0:T(128)S(1)} %reshape.77, f32[64,128,128]{2,1,0:T(8,128)} %copy.17), kind=kCustom, calls=%fused_computation.1 | custom fusion | flops 1048576 | bytes 12583168 | tf_op jit(solution)/shard_map/scatter-add | solution.py:38
  125.1 0.0 reduce-scatter.2.cloned.1.call-update
  125.2 107.2 %all-reduce.2.cloned.1.call-done = f32[128,256]{1,0:T(8,128)} async-done(((f32[128,256]{1,0:T(8,128)}), f32[128,256]{1,0:T(8,128)}) %all-reduce.2.cloned.1.call-update) | async-done | bytes 131088 | tf_op jit(solution)/shard_map/psum | solution.py:49
  232.3 1.3 constant_dynamic-slice_fusion
  233.6 666.3 %reduce-scatter.2.cloned.1.call-done = f32[256,128]{1,0:T(8,128)} async-done(((f32[32768,128]{1,0:T(8,128)}), f32[256,128]{1,0:T(8,128)}) %reduce-scatter.2.cloned.1.call-update) | async-done | bytes 131088 | tf_op jit(solution)/shard_map/reduce_scatter | solution.py:44
  (2 shorter events, 0.0 us)
Async XLA Ops:
  7.2 82.1 %copy-start = (bf16[2,32,128,128]{3,2,1,0:T(8,128)(2,1)S(1)}, bf16[2,32,128,128]{3,2,1,0:T(8,128)(2,1)}, u32[]{:S(2)}) copy-start(bf16[2,32,128,128]{3,2,1,0:T(8,128)(2,1)} %param.8) | copy-start | bytes 6291460
  7.2 76.4 %all-gather.2.cloned.1.call-start = ((), (), s32[]{:S(2)}) async-start(), calls=%async_computation.1 | async-start | bytes 8454144 | tf_op jit(solution)/shard_map/all_gather | solution.py:13
  7.9 224.4 %all-reduce.2.cloned.1.call-start = ((), (), s32[]{:S(2)}) async-start(), calls=%async_computation.3 | async-start | bytes 262144 | tf_op jit(solution)/shard_map/psum | solution.py:49
  83.6 8.9 copy-start.1
  83.6 8.9 copy-start.2
  94.6 805.3 %reduce-scatter.2.cloned.1.call-start = ((), (), s32[]{:S(2)}) async-start(), calls=%async_computation.2 | async-start | bytes 16908288 | tf_op jit(solution)/shard_map/reduce_scatter | solution.py:44
Sparse Core Ops, SparseCore 0:
  11.0 72.5 all-gather.1
  94.7 137.6 all-reduce.1
  235.4 664.3 reduce-scatter.1
where the time goes:
time: 907 us; the launch traced here: 906 us
  waiting for transfers between devices  848 us (93%)
  local copies, waits for them, and re-layouts  22 us (2%)
  other arithmetic  17 us (2%)
  between operations  13.8 us (2%)
    reduce_scatter x1, waiting for transfers between devices, on_device(): lax.psum_scatter(column_terms, 'dev', scatter_dimension=0, tiled=True)  666 us
    psum x1, waiting for transfers between devices, on_device(): weight_total = lax.psum(local_weight, 'dev')  107 us
    all_gather x1, waiting for transfers between devices, on_device(): gathered = lax.all_gather(features, 'dev', axis=0, tiled=True)  73.4 us
  transfers between devices with their start and end apart: 3, of which 3 were waited for; matrix products, arithmetic and copies ran while one was open for 4% of the time, Pallas kernels for 0%

commit v1 on v0

v1 whole, which is shorter than its diff:
```python
import functools

import jax
import jax.numpy as jnp
import numpy as np
from jax import lax
from jax.experimental import pallas as pl
from jax.experimental.pallas import tpu as pltpu
from jax.sharding import PartitionSpec as P

MESH = pl.DeviceIdType.MESH
BF16, F32 = jnp.bfloat16, jnp.float32
SIDE = 4
TILE, SLOTS, FIN, HID = 128, 32, 128, 256
BLOCKS = 256
ROWS = (48, 48, 32)
STARTS = (0, 48, 96)
EXTRA = 16
CHUNK = (96, 96, 80)
ORDER = ((0, 1, 2), (1, 2, 0), (2, 0, 1))
HOPS = (1, 3, 2)


def column_table():
    table = np.zeros((3, 2, SIDE, SIDE, SIDE, 2), np.int32)
    for part in range(3):
        for place in np.ndindex(table.shape[1:]):
            core, half = place[0], place[4]
            at = {axis: place[1 + n] for n, axis in enumerate(ORDER[part])}
            device = ((at[0] * SIDE + at[1]) * SIDE + at[2]) * 2 + core
            table[(part,) + place] = device * 2 + half
    return table.reshape(3, BLOCKS)


def place_of_column(cols, part):
    core, half = (cols >> 1) & 1, cols & 1
    at = (cols >> 6, (cols >> 4) & 3, (cols >> 2) & 3)
    flat = core
    for axis in ORDER[part]:
        flat = flat * SIDE + at[axis]
    return flat * 2 + half


def kernel(
    place_ref, slot_ref, features_hbm, weight_hbm, tiles_hbm, cotangent_hbm,
    act_ref, grad_ref, weight_grad_ref,
    x_ref, w_ref, tiles, ct_ref,
    f0, f1, f2, t0, t1, t2, out0, out1, out2, in0, in1, in2, own0, own1, own2,
    pass_up0, pass_up1, pass_up2, pass_down0, pass_down1, pass_down2,
    end_up0, end_up1, end_up2, end_down0, end_down1, end_down2,
    b0, b1, b2, rb0, rb1, rb2, c0, c1, c2, rc0, rc1, rc2, wg_ref,
    load_sem, g1s, g1r, g2s, g2r, g3s, g3r, gcs, gcr,
    xs, xr, pas, par, pes, per, bs, br, cs, cr,
):
    parts = range(3)
    gathered = (f0, f1, f2)
    terms = (t0, t1, t2)
    to_twin, from_twin, own = (out0, out1, out2), (in0, in1, in2), (own0, own1, own2)
    pass_up, pass_down = (pass_up0, pass_up1, pass_up2), (pass_down0, pass_down1, pass_down2)
    end_up, end_down = (end_up0, end_up1, end_up2), (end_down0, end_down1, end_down2)
    mid, mid_in = (b0, b1, b2), (rb0, rb1, rb2)
    last, last_in = (c0, c1, c2), (rc0, rc1, rc2)

    me = lax.axis_index("dev")
    core = me % 2
    at = (me // 32, (me // 8) % 4, (me // 2) % 4)

    def device(axis, hop):
        moved = [(at[a] + hop) % SIDE if a == axis else at[a] for a in range(3)]
        return (((moved[0] * SIDE + moved[1]) * SIDE + moved[2]) * 2 + core,)

    twin = (me + 1 - 2 * core,)

    loads = [
        pltpu.make_async_copy(src, dst, load_sem.at[n])
        for n, (src, dst) in enumerate(
            ((features_hbm, x_ref), (weight_hbm, w_ref), (tiles_hbm, tiles), (cotangent_hbm, ct_ref))
        )
    ]
    for load in loads:
        load.start()

    barrier = pltpu.get_barrier_semaphore()
    for axis in range(3):
        for hop in HOPS:
            pl.semaphore_signal(barrier, inc=1, device_id=device(axis, hop), device_id_type=MESH)
    pl.semaphore_signal(barrier, inc=1, device_id=twin, device_id_type=MESH)

    for p in parts:
        gathered[p][2 * BLOCKS // 2] = jnp.zeros((ROWS[p], FIN), BF16)
        terms[p][2 * SLOTS] = jnp.zeros((ROWS[p], TILE), BF16)

    def flat(p, slow, middle, fast):
        return (slow * SIDE + middle) * SIDE + fast

    i3 = [at[ORDER[p][0]] for p in parts]
    i2 = [at[ORDER[p][1]] for p in parts]
    i1 = [at[ORDER[p][2]] for p in parts]
    loads[0].wait()
    for p in parts:
        place = (core * 64 + flat(p, i3[p], i2[p], i1[p])) * 2
        for half in range(2):
            gathered[p][place + half] = x_ref[pl.ds(half * TILE + STARTS[p], ROWS[p]), :]

    pl.semaphore_wait(barrier, 10)

    sends = []

    def send(src, dst, ssem, rsem, to):
        copy = pltpu.make_async_remote_copy(
            src_ref=src, dst_ref=dst, send_sem=ssem, recv_sem=rsem, device_id=to, device_id_type=MESH
        )
        copy.start()
        sends.append(copy)

    def arrived(dst, ssem, rsem):
        pltpu.make_async_remote_copy(
            src_ref=dst, dst_ref=dst, send_sem=ssem, recv_sem=rsem, device_id=twin, device_id_type=MESH
        ).wait_recv()

    def chunk(p, slow, middle, fast, count=1):
        return gathered[p].at[pl.ds((core * 64 + flat(p, slow, middle, fast)) * 2, 2 * count)]

    for p in parts:
        mine = chunk(p, i3[p], i2[p], i1[p])
        for n, hop in enumerate(HOPS):
            send(mine, mine, g1s.at[p, n], g1r.at[p, n], device(ORDER[p][2], hop))
    for r in range(4):
        for p in parts:
            fast = i1[p] if r == 0 else (i1[p] + SIDE - HOPS[r - 1]) % SIDE
            ref = chunk(p, i3[p], i2[p], fast)
            if r > 0:
                arrived(ref, g1s.at[p, r - 1], g1r.at[p, r - 1])
            for n, hop in enumerate(HOPS):
                send(ref, ref, g2s.at[p, r * 3 + n], g2r.at[p, r * 3 + n], device(ORDER[p][1], hop))

    def slab(p, slow, r):
        middle = i2[p] if r == 0 else (i2[p] + SIDE - HOPS[r - 1]) % SIDE
        return chunk(p, slow, middle, 0, SIDE)

    def to_the_twin(p, ref, n):
        send(ref, ref, gcs.at[p, n], gcr.at[p], twin)

    def pass_on(p, r):
        up = slab(p, (i3[p] + 3) % SIDE, r)
        down = slab(p, (i3[p] + 1) % SIDE, r)
        arrived(up, g3s.at[p, 2 * r], g3r.at[p, 2 * r])
        if r < 2:
            send(up, up, g3s.at[p, 8 + r], g3r.at[p, 8 + r], device(ORDER[p][0], 1))
        to_the_twin(p, up, 4 + 2 * r)
        arrived(down, g3s.at[p, 2 * r + 1], g3r.at[p, 2 * r + 1])
        if r >= 2:
            send(down, down, g3s.at[p, 8 + r], g3r.at[p, 8 + r], device(ORDER[p][0], 3))
        to_the_twin(p, down, 5 + 2 * r)

    for r in range(4):
        for p in parts:
            ref = slab(p, i3[p], r)
            if r > 0:
                middle = (i2[p] + SIDE - HOPS[r - 1]) % SIDE
                for s in range(4):
                    fast = i1[p] if s == 0 else (i1[p] + SIDE - HOPS[s - 1]) % SIDE
                    n = s * 3 + r - 1
                    arrived(chunk(p, i3[p], middle, fast), g2s.at[p, n], g2r.at[p, n])
            send(ref, ref, g3s.at[p, 2 * r], g3r.at[p, 2 * r], device(ORDER[p][0], 1))
            send(ref, ref, g3s.at[p, 2 * r + 1], g3r.at[p, 2 * r + 1], device(ORDER[p][0], 3))
            to_the_twin(p, ref, r)
        if r > 0:
            for p in parts:
                pass_on(p, r - 1)
    for p in parts:
        pass_on(p, 3)
    for r in range(4):
        for p in parts:
            ref = slab(p, (i3[p] + 2) % SIDE, r)
            arrived(ref, g3s.at[p, 8 + r], g3r.at[p, 8 + r])
            to_the_twin(p, ref, 12 + r)
    for load in loads[1:]:
        load.wait()
    for p in parts:
        arrived(gathered[p].at[pl.ds((1 - core) * 128, 128)], gcs.at[p, 0], gcr.at[p])

    def block_of(slot):
        return jnp.concatenate([gathered[p][place_ref[p, slot]] for p in parts], axis=0)

    def forward_step(n, totals):
        new = []
        for b in range(2):
            total = totals[b]
            for k in range(2):
                slot = n * 4 + k * 2
                left = jnp.concatenate([tiles[b, slot], tiles[b, slot + 1]], axis=1)
                right = jnp.concatenate([block_of(b * SLOTS + slot), block_of(b * SLOTS + slot + 1)], axis=0)
                total = total + jnp.dot(left, right, preferred_element_type=F32)
            new.append(total)
        return tuple(new)

    zero = jnp.zeros((TILE, FIN), F32)
    totals = lax.fori_loop(0, SLOTS // 4, forward_step, (zero, zero))
    aggregated = jnp.concatenate(totals, axis=0).astype(BF16)
    weight = w_ref[...]
    pre = jnp.dot(aggregated, weight, preferred_element_type=F32)
    sigma = jax.nn.sigmoid(pre)
    act_ref[...] = (pre * sigma).astype(BF16)
    delta = (ct_ref[...].astype(F32) * sigma * (1.0 + pre * (1.0 - sigma))).astype(BF16)
    back = lax.dot_general(
        weight, delta, (((1,), (1,)), ((), ())), preferred_element_type=F32
    ).astype(BF16)
    weight_terms = lax.dot_general(
        aggregated, delta, (((0,), (0,)), ((), ())), preferred_element_type=F32
    )
    for half in range(2):
        wg_ref[pl.ds(half * FIN, FIN), :] = weight_terms[:, half * TILE : (half + 1) * TILE]

    for b in range(2):
        left = back[:, b * TILE : (b + 1) * TILE]

        def term_step(n, carry, b=b, left=left):
            for k in range(2):
                slot = n * 4 + k * 2
                right = jnp.concatenate([tiles[b, slot], tiles[b, slot + 1]], axis=1)
                both = jnp.dot(left, right, preferred_element_type=F32).astype(BF16)
                for half in range(2):
                    for p in parts:
                        terms[p][b * SLOTS + slot + half] = both[
                            STARTS[p] : STARTS[p] + ROWS[p], half * TILE : (half + 1) * TILE
                        ]
            return carry

        lax.fori_loop(0, SLOTS // 4, term_step, 0)

    row = lax.broadcasted_iota(jnp.int32, (EXTRA, TILE), 0)

    def weight_rows(p, which, position):
        slow, middle, fast = position // 16, (position // 4) % 4, position % 4
        moved = {ORDER[p][0]: slow, ORDER[p][1]: middle, ORDER[p][2]: fast}
        target = ((moved[0] * SIDE + moved[1]) * SIDE + moved[2]) * 2 + which
        first = wg_ref[pl.ds(target, 1), :]
        second = wg_ref[pl.ds(FIN + target, 1), :]
        return jnp.where(row == 0, first, jnp.where(row == 1, second, 0.0)).astype(BF16)

    def spread(p, which, slow, dst, extra):
        def step(n, carry):
            values = []
            for k in range(2):
                position = slow * 16 + n * 2 + k
                halves = []
                for half in range(2):
                    entry = (which * 64 + position) * 2 + half
                    halves.append(terms[p][slot_ref[p, 0, entry]] + terms[p][slot_ref[p, 1, entry]])
                if p == 2:
                    halves.append(weight_rows(p, which, position))
                value = jnp.concatenate(halves, axis=0)
                if extra is not None:
                    value = value + extra[position]
                values.append((position, value))
            for position, value in values:
                dst[position] = value
            return carry

        lax.fori_loop(0, 8, step, 0)

    away = (2, 1, 3, 0)
    for n, o in enumerate(away):
        for p in parts:
            slow = (i3[p] + o) % SIDE
            spread(p, 1 - core, slow, to_twin[p], None)
            send(
                to_twin[p].at[pl.ds(slow * 16, 16)], from_twin[p].at[pl.ds(slow * 16, 16)],
                xs.at[p, n], xr.at[p, n], twin,
            )

    def part_of(ref, slow, middle):
        return ref.at[pl.ds(slow * 16 + middle * 4, 4)]

    def slab_at(p, q):
        return (i2[p] + away[q]) % SIDE

    for n, o in enumerate(away):
        for p in parts:
            slow = (i3[p] + o) % SIDE
            ref = from_twin[p].at[pl.ds(slow * 16, 16)]
            arrived(ref, xs.at[p, n], xr.at[p, n])
            spread(p, core, slow, own[p], from_twin[p])
            up, down = device(ORDER[p][0], 1), device(ORDER[p][0], 3)
            if o == 2:
                for q in range(2):
                    send(part_of(own[p], slow, slab_at(p, q)), pass_up[p].at[q], pas.at[p, q], par.at[p, q], up)
                    send(
                        part_of(own[p], slow, slab_at(p, q + 2)), pass_down[p].at[q],
                        pas.at[p, 2 + q], par.at[p, 2 + q], down,
                    )
            if o == 1:
                for q in range(2, 4):
                    send(part_of(own[p], slow, slab_at(p, q)), end_up[p].at[q], pes.at[p, q], per.at[p, q], up)
            if o == 3:
                for q in range(2):
                    send(
                        part_of(own[p], slow, slab_at(p, q)), end_down[p].at[q],
                        pes.at[p, 4 + q], per.at[p, 4 + q], down,
                    )
    for q in range(2):
        for p in parts:
            up, down = device(ORDER[p][0], 1), device(ORDER[p][0], 3)
            arrived(pass_up[p].at[q], pas.at[p, q], par.at[p, q])
            ref = part_of(own[p], (i3[p] + 1) % SIDE, slab_at(p, q))
            ref[...] = ref[...] + pass_up[p][q]
            send(ref, end_up[p].at[q], pes.at[p, q], per.at[p, q], up)
            arrived(pass_down[p].at[q], pas.at[p, 2 + q], par.at[p, 2 + q])
            ref = part_of(own[p], (i3[p] + 3) % SIDE, slab_at(p, q + 2))
            ref[...] = ref[...] + pass_down[p][q]
            send(ref, end_down[p].at[q + 2], pes.at[p, 6 + q], per.at[p, 6 + q], down)
    for q in range(4):
        for p in parts:
            arrived(end_up[p].at[q], pes.at[p, q], per.at[p, q])
            arrived(end_down[p].at[q], pes.at[p, 4 + q], per.at[p, 4 + q])
            ref = part_of(own[p], i3[p], slab_at(p, q))
            total = ref[...].astype(F32) + end_up[p][q].astype(F32) + end_down[p][q].astype(F32)
            mid[p][q] = total.astype(BF16)
            if q < 3:
                send(mid[p].at[q], mid_in[p].at[q], bs.at[p, q], br.at[p, q], device(ORDER[p][1], away[q]))
    for p in parts:
        for q in range(3):
            arrived(mid_in[p].at[q], bs.at[p, q], br.at[p, q])
        total = mid[p][3].astype(F32)
        for q in range(3):
            total = total + mid_in[p][q].astype(F32)
        last[p][...] = total.astype(BF16)
        for q in range(3):
            place = (i1[p] + away[q]) % SIDE
            send(last[p].at[place], last_in[p].at[q], cs.at[p, q], cr.at[p, q], device(ORDER[p][2], away[q]))
    results = []
    for p in parts:
        for q in range(3):
            arrived(last_in[p].at[q], cs.at[p, q], cr.at[p, q])
        total = last[p][i1[p]].astype(F32)
        for q in range(3):
            total = total + last_in[p][q].astype(F32)
        results.append(total)
    for half in range(2):
        block = jnp.concatenate(
            [results[p][half * ROWS[p] : (half + 1) * ROWS[p]] for p in parts], axis=0
        )
        grad_ref[pl.ds(half * TILE, TILE), :] = block.T
    weight_grad_ref[:, pl.ds(0, TILE)] = results[2][64:65]
    weight_grad_ref[:, pl.ds(TILE, TILE)] = results[2][65:66]
    for copy in sends:
        copy.wait_send()


def on_device(features, weight, tile_values, tile_cols, tile_counts, cotangent):
    live = tile_counts > 0
    cols = tile_cols.reshape(-1)
    place = jnp.stack(
        [jnp.where(live.reshape(-1), place_of_column(cols, p), BLOCKS) for p in range(3)]
    )
    table = jnp.asarray(column_table())
    slot = jnp.arange(2 * SLOTS, dtype=jnp.int32).reshape(2, SLOTS)
    hit = (table[:, None, :, None] == tile_cols[None, :, None, :]) & live[None, :, None, :]
    slots = 2 * SLOTS + jnp.sum(jnp.where(hit, slot[None, :, None, :] - 2 * SLOTS, 0), axis=3)

    def vmem(*shape, dtype=BF16):
        return pltpu.VMEM(shape, dtype)

    def three(*lead, rows, lanes=128):
        return [vmem(*lead, rows[p], lanes) for p in range(3)]

    dma = pltpu.SemaphoreType.DMA
    smem, anywhere, in_vmem = (
        pl.BlockSpec(memory_space=pltpu.SMEM),
        pl.BlockSpec(memory_space=pl.ANY),
        pl.BlockSpec(memory_space=pltpu.VMEM),
    )
    scratch = (
        [vmem(256, FIN), vmem(FIN, HID), vmem(2, SLOTS, TILE, TILE), vmem(256, HID)]
        + three(BLOCKS + 1, rows=ROWS)
        + three(2 * SLOTS + 1, rows=ROWS)
        + three(64, rows=CHUNK)
        + three(64, rows=CHUNK)
        + three(64, rows=CHUNK)
        + three(2, 4, rows=CHUNK)
        + three(2, 4, rows=CHUNK)
        + three(4, 4, rows=CHUNK)
        + three(4, 4, rows=CHUNK)
        + three(4, 4, rows=CHUNK)
        + three(3, 4, rows=CHUNK)
        + three(4, rows=CHUNK)
        + three(3, rows=CHUNK)
        + [vmem(2 * FIN, TILE, dtype=F32)]
        + [dma((4,))]
        + [dma((3, 3)), dma((3, 3)), dma((3, 12)), dma((3, 12)), dma((3, 12)), dma((3, 12)), dma((3, 16)), dma((3,))]
        + [dma((3, 4)), dma((3, 4)), dma((3, 4)), dma((3, 4)), dma((3, 8)), dma((3, 8))]
        + [dma((3, 3)), dma((3, 3)), dma((3, 3)), dma((3, 3))]
    )
    return pl.pallas_call(
        kernel,
        out_shape=(
            jax.ShapeDtypeStruct((256, HID), BF16),
            jax.ShapeDtypeStruct((256, FIN), F32),
            jax.ShapeDtypeStruct((1, HID), F32),
        ),
        in_specs=[smem, smem, anywhere, anywhere, anywhere, anywhere],
        out_specs=(in_vmem, in_vmem, in_vmem),
        scratch_shapes=scratch,
        compiler_params=pltpu.CompilerParams(
            collective_id=0, has_side_effects=True, vmem_limit_bytes=56 << 20
        ),
        name="graph_layer",
    )(place, slots, features, weight, tile_values, cotangent)


def solution(mesh):
    return jax.shard_map(
        on_device,
        mesh=mesh,
        in_specs=(
            P("dev", None),
            P(),
            P("dev", None, None, None),
            P("dev", None),
            P("dev", None),
            P("dev", None),
        ),
        out_specs=(P("dev", None), P("dev", None), P("dev", None)),
        check_vma=False,
    )
```

time: 907 us -> 81.3 us (0.09)
  waiting for transfers between devices: 848 us -> 0 us
  Pallas kernels: 0 us -> 71.9 us
  local copies, waits for them, and re-layouts: 22 us -> 4.86 us
  other arithmetic: 17 us -> 3.4 us
  between operations: 13.8 us -> 0.65 us
    reduce_scatter x1 -> x0, waiting for transfers between devices: 666 us -> none  [on_device(): lax.psum_scatter(column_terms, 'dev', scatter_dimension=0, tiled=True)]
    psum x1 -> x0, waiting for transfers between devices: 107 us -> none  [on_device(): weight_total = lax.psum(local_weight, 'dev')]
    all_gather x1 -> x0, waiting for transfers between devices: 73.4 us -> none  [on_device(): gathered = lax.all_gather(features, 'dev', axis=0, tiled=True)]
    pallas_call x0 -> x1, Pallas kernels: none -> 71.9 us  [on_device(): pl.pallas_call(kernel, out_shape=(jax.ShapeDtypeStruct((256, HID), BF16),...]
    scatter-add x1 -> x0, other arithmetic: 13.7 us -> none  [on_device(): jax.ops.segment_sum(widened.reshape(-1, tile_size, in_width), tile_cols.r...]
  transfers between devices with their start and end apart: 3 -> 0, of which waited for: 3 -> 0; matrix products, arithmetic and copies ran while one was open for 4% -> 0% of each run, Pallas kernels for 0% -> 0%
where the time goes in v1:
time: 81.3 us; the launch traced here: 80.8 us
  Pallas kernels  71.9 us (88%)
  local copies, waits for them, and re-layouts  4.86 us (6%)
  other arithmetic  3.4 us (4%)
    pallas_call x1, Pallas kernels, on_device(): pl.pallas_call(kernel, out_shape=(jax.ShapeDtypeStruct((256, HID), BF16),...  71.9 us
    unnamed x3, local copies, waits for them, and re-layouts  4.37 us

profile of v1, /device:TPU:0, one launch (start us, length us, event | category | flops | bytes accessed | tf_op | source)
XLA Modules:
  0.0 80.8 jit_solution(17834236729234457417)
XLA Ops:
  0.6 0.7 broadcast_compare_fusion
  1.3 0.1 reshape.231
  1.4 0.8 %select_reduce_fusion = s32[3,2,256]{2,1,0:T(2,128)S(1)} fusion(s32[2,32]{1,0:T(2,128)S(1)} %add_add_fusion, s32[2,32]{1,0:T(2,128)} %param.10, s32[3,256]{1,0:T(4,128)} %constant.26.clone, pred[2,32]{1,0:T(4,128)(4,1)S(1)} %broadcast_compare_fusion), kind=kLoop, calls=%fused_computation | loop fusion | flops 195072 | bytes 9792 | tf_op jit(solution)/shard_map/reduce_sum | solution.py:360
  2.2 0.6 broadcast_add_fusion.slot_ref
  2.8 0.7 shift-right-arithmetic_and_fusion
  3.5 0.1 and.102
  3.6 0.1 and.100
  3.7 0.1 shift_right_arithmetic.88
  3.8 0.1 mul.114
  3.9 0.1 and.104
  3.9 0.6 pad_add_fusion.place_ref
  4.5 71.9 %graph_layer.1 = (bf16[256,256]{1,0:T(8,128)(2,1)}, f32[256,128]{1,0:T(8,128)}, f32[1,256]{1,0:T(1,128)}) custom-call(s32[3,64]{1,0:T(4,128)} %pad_add_fusion.place_ref, s32[3,2,256]{2,1,0:T(2,128)} %broadcast_add_fusion.slot_ref, bf16[256,128]{1,0:T(8,128)(2,1)} %features_hbm.1, bf16[128,256]{1,0:T(8,128)(2,1)} %weight_hbm.1, ...), custom_call_target="tpu_custom_call" | custom-call | tf_op jit(solution)/shard_map/graph_layer/pallas_call | solution.py:395
  76.4 1.6 %copy.13 = bf16[256,256]{1,0:T(8,128)(2,1)} copy(bf16[256,256]{1,0:T(8,128)(2,1)} %get-tuple-element.14) | data formatting | bytes 262144
  78.0 1.6 %copy.14 = f32[256,128]{1,0:T(8,128)} copy(f32[256,128]{1,0:T(8,128)} %get-tuple-element.15) | data formatting | bytes 262144
  79.6 1.2 %copy.15 = f32[1,256]{1,0:T(1,128)} copy(f32[1,256]{1,0:T(1,128)} %get-tuple-element.16) | data formatting | bytes 2048
  (2 shorter events, 0.0 us)

commit v2 on v0

v2 whole, which is shorter than its diff:
```python
import jax
import jax.numpy as jnp
from jax import lax
from jax.experimental import pallas as pl
from jax.experimental.pallas import tpu as pltpu
from jax.sharding import PartitionSpec as P

MESH = pl.DeviceIdType.MESH
BF16, F32, I32 = jnp.bfloat16, jnp.float32, jnp.int32
SIDE = 4
TILE, SLOTS, FIN, HID = 128, 32, 128, 256
CHUNKS = 64
UNIT = 16
UNITS = (6, 5, 5)
BASE = (0, 129 * 6, 129 * 11)
ROWS = (48, 48, 32)
STARTS = (0, 48, 96)
EXTRA = 16
CHUNK = (96, 96, 80)
NONE = 4 * SLOTS
ORDER = ((0, 1, 2), (1, 2, 0), (2, 0, 1))
HOPS = (1, 3, 2)


def pick(which, values):
    return jnp.where(which == 0, values[0], jnp.where(which == 1, values[1], values[2]))


def kernel(
    features_hbm, weight_hbm, tiles_hbm, cols_hbm, counts_hbm, cotangent_hbm,
    act_hbm, grad_ref, weight_grad_ref,
    gathered, w_ref, tiles, ct_ref, cols_ref, counts_ref, cols_smem, counts_smem, act_ref,
    place_ref, place_smem, slot_ref, twin_slot_out, twin_slot_ref, slot_smem, t0, t1, t2, own0, own1, own2,
    pass_up0, pass_up1, pass_up2, pass_down0, pass_down1, pass_down2,
    end_up0, end_up1, end_up2, end_down0, end_down1, end_down2,
    b0, b1, b2, rb0, rb1, rb2, c0, c1, c2, rc0, rc1, rc2, wg_ref, twin_wg_ref,
    load_sem, act_sem, table_sem, g1s, g1r, g2s, g2r, gos, gor, g3s, g3r, gcs, gcr, ts, tr, es, er,
    pas, par, pes, per, bs, br, cs, cr,
):
    parts = range(3)
    terms, own = (t0, t1, t2), (own0, own1, own2)
    pass_up, pass_down = (pass_up0, pass_up1, pass_up2), (pass_down0, pass_down1, pass_down2)
    end_up, end_down = (end_up0, end_up1, end_up2), (end_down0, end_down1, end_down2)
    mid, mid_in = (b0, b1, b2), (rb0, rb1, rb2)
    last, last_in = (c0, c1, c2), (rc0, rc1, rc2)

    me = lax.axis_index("dev")
    core = me % 2
    at = (me // 32, (me // 8) % 4, (me // 2) % 4)
    strides = (32, 8, 2)

    def device(axis, hop):
        return (me + ((at[axis] + hop) % SIDE - at[axis]) * strides[axis],)

    twin = (me + 1 - 2 * core,)

    barrier = pltpu.get_barrier_semaphore()
    for hop in (2, 1, 3):
        for axis in range(3):
            pl.semaphore_signal(barrier, inc=1, device_id=device(axis, hop), device_id_type=MESH)
    pl.semaphore_signal(barrier, inc=1, device_id=twin, device_id_type=MESH)

    turn = [(core + p) % 3 for p in parts]
    i3, i2, i1 = ([pick((turn[p] + n) % 3, at) for p in parts] for n in range(3))
    s3, s2, s1 = ([pick((turn[p] + n) % 3, strides) for p in parts] for n in range(3))

    def move(index, stride, hop):
        return (me + ((index + hop) % SIDE - index) * stride,)

    def chunk(p, slow, middle, fast, count=1):
        at_chunk = core * CHUNKS + (slow * SIDE + middle) * SIDE + fast
        return gathered.at[pl.ds(BASE[p] + at_chunk * UNITS[p], count * UNITS[p])]

    loads = []

    def load(src, dst):
        copy = pltpu.make_async_copy(src, dst, load_sem.at[len(loads)])
        copy.start()
        loads.append(copy)

    for p, first, unit, count in ((0, 0, 0, 3), (1, 3, 0, 3), (2, 6, 0, 2), (0, 8, 3, 3), (1, 11, 3, 2), (2, 13, 2, 3)):
        place = BASE[p] + (core * CHUNKS + (i3[p] * SIDE + i2[p]) * SIDE + i1[p]) * UNITS[p] + unit
        load(features_hbm.at[pl.ds(first, count)], gathered.at[pl.ds(place, count)])
    load(cols_hbm, cols_smem)
    load(counts_hbm, counts_smem)
    load(cols_hbm, cols_ref)
    load(counts_hbm, counts_ref)
    load(tiles_hbm, tiles)
    load(weight_hbm, w_ref)
    load(cotangent_hbm, ct_ref)

    sends = []

    def send(src, dst, ssem, rsem, to):
        copy = pltpu.make_async_remote_copy(
            src_ref=src, dst_ref=dst, send_sem=ssem, recv_sem=rsem, device_id=to, device_id_type=MESH
        )
        copy.start()
        sends.append(copy)

    def arrived(dst, ssem, rsem):
        pltpu.make_async_remote_copy(
            src_ref=dst, dst_ref=dst, send_sem=ssem, recv_sem=rsem, device_id=twin, device_id_type=MESH
        ).wait_recv()

    for copy in loads[:6]:
        copy.wait()
    pl.semaphore_wait(barrier, 10)

    def first_sends(p, r):
        fast = i1[p] if r == 0 else (i1[p] + SIDE - HOPS[r - 1]) % SIDE
        ref = chunk(p, i3[p], i2[p], fast)
        if r > 0:
            arrived(ref, g1s.at[p, r - 1], g1r.at[p, r - 1])
        for n, hop in enumerate(HOPS):
            send(ref, ref, g2s.at[p, r * 3 + n], g2r.at[p, r * 3 + n], move(i2[p], s2[p], hop))
        return ref

    for p in parts:
        mine = chunk(p, i3[p], i2[p], i1[p])
        for n, hop in enumerate(HOPS):
            send(mine, mine, g1s.at[p, n], g1r.at[p, n], move(i1[p], s1[p], hop))
    for r in range(4):
        refs = [first_sends(p, r) for p in parts]
        for p in parts:
            for n, hop in enumerate((1, 3)):
                k = r * 2 + n
                send(refs[p], refs[p], gos.at[p, k], gor.at[p, k], move(i3[p], s3[p], hop))

    def slab(p, slow, r):
        middle = i2[p] if r == 0 else (i2[p] + SIDE - HOPS[r - 1]) % SIDE
        return chunk(p, slow, middle, 0, SIDE)

    def to_the_twin(p, ref, n):
        send(ref, ref, gcs.at[p, n], gcr.at[p], twin)

    def slab_arrived(p, r, slow, n):
        ref = slab(p, slow, r)
        if r == 0:
            for s in range(4):
                fast = i1[p] if s == 0 else (i1[p] + SIDE - HOPS[s - 1]) % SIDE
                arrived(chunk(p, slow, i2[p], fast), gos.at[p, s * 2 + n], gor.at[p, s * 2 + n])
        else:
            arrived(ref, g3s.at[p, 2 * r + n], g3r.at[p, 2 * r + n])
        return ref

    def pass_on(p, r):
        up = slab_arrived(p, r, (i3[p] + 3) % SIDE, 0)
        if r < 2:
            send(up, up, g3s.at[p, 8 + r], g3r.at[p, 8 + r], move(i3[p], s3[p], 1))
        to_the_twin(p, up, 4 + 2 * r)
        down = slab_arrived(p, r, (i3[p] + 1) % SIDE, 1)
        if r >= 2:
            send(down, down, g3s.at[p, 8 + r], g3r.at[p, 8 + r], move(i3[p], s3[p], 3))
        to_the_twin(p, down, 5 + 2 * r)

    for p in parts:
        to_the_twin(p, slab(p, i3[p], 0), 0)

    for p in parts:
        gathered[pl.ds(BASE[p] + 2 * CHUNKS * UNITS[p], UNITS[p])] = jnp.zeros((UNITS[p], UNIT, FIN), BF16)
        terms[p][NONE] = jnp.zeros((ROWS[p], TILE), BF16)
    for copy in loads[6:]:
        copy.wait()
    cols = cols_ref[...]
    live = counts_ref[...] > 0
    where = (cols >> 6, (cols >> 4) & 3, (cols >> 2) & 3)
    col_core, half = (cols >> 1) & 1, jnp.where(live, cols & 1, 0)
    starts = []
    for p in parts:
        turned = (col_core + p) % 3
        flat = col_core
        for n in range(3):
            flat = flat * SIDE + pick((turned + n) % 3, where)
        starts.append(BASE[p] + jnp.where(live, flat, 2 * CHUNKS) * UNITS[p])
    place_ref[0] = starts[0] + 3 * half
    place_ref[1] = starts[1] + 3 * half
    place_ref[2] = jnp.where(half == 0, starts[1], starts[2]) + 2
    place_ref[3] = starts[2] + 3 * half
    place_copy = pltpu.make_async_copy(place_ref, place_smem, table_sem.at[0])
    place_copy.start()
    line = lax.broadcasted_iota(I32, (8, TILE), 0)
    lane = lax.broadcasted_iota(I32, (8, TILE), 1)
    digits = (lane >> 5, (lane >> 3) & 3, (lane >> 1) & 3)
    column = 0
    for axis in range(3):
        digit = pick(line & 3, [digits[ORDER[p].index(axis)] for p in parts])
        column = column * SIDE + digit
    column = column * 4 + (line >> 2) * 2 + (lane & 1)
    for b in range(2):
        def find(s, found, b=b):
            wanted = jnp.where(counts_smem[b, s] > 0, cols_smem[b, s], -1)
            return jnp.where(column == wanted, b * SLOTS + s, found)

        found = lax.fori_loop(0, SLOTS, find, jnp.full((8, TILE), NONE, I32))
        slot_ref[b] = found
        twin_slot_out[b] = jnp.where(found < NONE, found + 2 * SLOTS, NONE)
    send(twin_slot_out, twin_slot_ref, es.at[0], er.at[0], twin)
    slot_copy = pltpu.make_async_copy(slot_ref, slot_smem.at[pl.ds(0, 2)], table_sem.at[1])
    slot_copy.start()

    for r in range(1, 4):
        for p in parts:
            ref = slab(p, i3[p], r)
            middle = (i2[p] + SIDE - HOPS[r - 1]) % SIDE
            for s in range(4):
                fast = i1[p] if s == 0 else (i1[p] + SIDE - HOPS[s - 1]) % SIDE
                n = s * 3 + r - 1
                arrived(chunk(p, i3[p], middle, fast), g2s.at[p, n], g2r.at[p, n])
            send(ref, ref, g3s.at[p, 2 * r], g3r.at[p, 2 * r], move(i3[p], s3[p], 1))
            send(ref, ref, g3s.at[p, 2 * r + 1], g3r.at[p, 2 * r + 1], move(i3[p], s3[p], 3))
            to_the_twin(p, ref, r)
        for p in parts:
            pass_on(p, r - 1)
    for p in parts:
        pass_on(p, 3)
    for r in range(4):
        for p in parts:
            ref = slab(p, (i3[p] + 2) % SIDE, r)
            arrived(ref, g3s.at[p, 8 + r], g3r.at[p, 8 + r])
            to_the_twin(p, ref, 12 + r)
    place_copy.wait()
    slot_copy.wait()
    arrived(twin_slot_ref, es.at[0], er.at[0])
    twin_slot_copy = pltpu.make_async_copy(twin_slot_ref, slot_smem.at[pl.ds(2, 2)], table_sem.at[2])
    twin_slot_copy.start()
    for p in parts:
        arrived(
            gathered.at[pl.ds(BASE[p] + (1 - core) * CHUNKS * UNITS[p], CHUNKS * UNITS[p])], gcs.at[p, 0], gcr.at[p]
        )

    def block_of(b, slot):
        pieces = [
            gathered[pl.ds(place_smem[0, b, slot], 3)].reshape(3 * UNIT, FIN),
            gathered[pl.ds(place_smem[1, b, slot], 2)].reshape(2 * UNIT, FIN),
            gathered[place_smem[2, b, slot]],
            gathered[pl.ds(place_smem[3, b, slot], 2)].reshape(2 * UNIT, FIN),
        ]
        return jnp.concatenate(pieces, axis=0)

    def forward_step(n, totals):
        new = []
        for b in range(2):
            total = totals[b]
            for k in range(FORWARD_UNROLL):
                slot = (n * FORWARD_UNROLL + k) * 2
                left = jnp.concatenate([tiles[b, slot], tiles[b, slot + 1]], axis=1)
                right = jnp.concatenate([block_of(b, slot), block_of(b, slot + 1)], axis=0)
                total = total + jnp.dot(left, right, preferred_element_type=F32)
            new.append(total)
        return tuple(new)

    zero = jnp.zeros((TILE, FIN), F32)
    totals = lax.fori_loop(0, SLOTS // (2 * FORWARD_UNROLL), forward_step, (zero, zero))
    aggregated = jnp.concatenate(totals, axis=0).astype(BF16)
    weight = w_ref[...]
    pre = jnp.dot(aggregated, weight, preferred_element_type=F32)
    sigma = jax.nn.sigmoid(pre)
    act_ref[...] = (pre * sigma).astype(BF16)
    act_copy = pltpu.make_async_copy(act_ref, act_hbm, act_sem)
    act_copy.start()
    delta = (ct_ref[...].astype(F32) * sigma * (1.0 + pre * (1.0 - sigma))).astype(BF16)
    back = lax.dot_general(
        weight, delta, (((1,), (1,)), ((), ())), preferred_element_type=F32
    ).astype(BF16)

    for b in range(2):
        left_factor = back[:, b * TILE : (b + 1) * TILE]
        for group in range(2):
            def term_step(n, carry, b=b, group=group, left_factor=left_factor):
                for k in range(TERM_UNROLL):
                    slot = group * 16 + (n * TERM_UNROLL + k) * 2
                    right = jnp.concatenate([tiles[b, slot], tiles[b, slot + 1]], axis=1)
                    both = jnp.dot(left_factor, right, preferred_element_type=F32).astype(BF16)
                    for which in range(2):
                        for p in parts:
                            terms[p][b * SLOTS + slot + which] = both[
                                STARTS[p] : STARTS[p] + ROWS[p], which * TILE : (which + 1) * TILE
                            ]
                return carry

            lax.fori_loop(0, 8 // TERM_UNROLL, term_step, 0)
            for p in parts:
                first = b * SLOTS + group * 16
                n = b * 2 + group
                send(
                    terms[p].at[pl.ds(first, 16)], terms[p].at[pl.ds(2 * SLOTS + first, 16)],
                    ts.at[p, n], tr.at[p, n], twin,
                )
    weight_terms = lax.dot_general(
        aggregated, delta, (((0,), (0,)), ((), ())), preferred_element_type=F32
    )
    for which in range(2):
        wg_ref[pl.ds(which * FIN, FIN), :] = weight_terms[:, which * TILE : (which + 1) * TILE]
    send(wg_ref, twin_wg_ref, es.at[1], er.at[1], twin)
    twin_slot_copy.wait()
    for p in parts:
        for n in range(4):
            arrived(terms[p].at[pl.ds(2 * SLOTS + n * 16, 16)], ts.at[p, n], tr.at[p, n])
    arrived(twin_wg_ref, es.at[1], er.at[1])

    row = lax.broadcasted_iota(I32, (EXTRA, TILE), 0)

    def weight_rows(p, slow, middle, fast):
        moved = {ORDER[p][0]: slow, ORDER[p][1]: middle, ORDER[p][2]: fast}
        target = ((moved[0] * SIDE + moved[1]) * SIDE + moved[2]) * 2 + core
        rows = []
        for which in range(2):
            place = pl.ds(which * FIN + target, 1)
            rows.append(wg_ref[place, :] + twin_wg_ref[place, :])
        return jnp.where(row == 0, rows[0], jnp.where(row == 1, rows[1], 0.0)).astype(BF16)

    def spread(p, slow, middle, dst, extras):
        values = []
        for fast in range(SIDE):
            halves = []
            for which in range(2):
                entry = ((slow * SIDE + middle) * SIDE + fast) * 2 + which
                found = [terms[p][slot_smem[k, core * 4 + p, entry]] for k in range(4)]
                halves.append((found[0] + found[1]) + (found[2] + found[3]))
            if p == 2:
                halves.append(weight_rows(p, slow, middle, fast))
            value = jnp.concatenate(halves, axis=0)
            if extras:
                value = value.astype(F32)
                for extra in extras:
                    value = value + extra[fast].astype(F32)
                value = value.astype(BF16)
            values.append(value)
        for fast in range(SIDE):
            dst[fast] = values[fast]

    away = (2, 1, 3, 0)

    def middle_at(p, q):
        return (at[ORDER[p][1]] + away[q]) % SIDE

    def own_slab(p, o, q, extras=()):
        slow, middle = (at[ORDER[p][0]] + o) % SIDE, middle_at(p, q)
        ref = own[p].at[pl.ds((slow * SIDE + middle) * SIDE, SIDE)]
        spread(p, slow, middle, ref, extras)
        return ref

    up = [device(ORDER[p][0], 1) for p in parts]
    down = [device(ORDER[p][0], 3) for p in parts]
    for q in (0, 2, 1, 3):
        for p in parts:
            ref = own_slab(p, 2, q)
            if q < 2:
                send(ref, pass_up[p].at[q], pas.at[p, q], par.at[p, q], up[p])
            else:
                send(ref, pass_down[p].at[q - 2], pas.at[p, q], par.at[p, q], down[p])
    for q in range(2):
        for p in parts:
            send(own_slab(p, 1, q + 2), end_up[p].at[q + 2], pes.at[p, q + 2], per.at[p, q + 2], up[p])
            send(own_slab(p, 3, q), end_down[p].at[q], pes.at[p, 4 + q], per.at[p, 4 + q], down[p])
    for q in range(2):
        for p in parts:
            arrived(pass_up[p].at[q], pas.at[p, q], par.at[p, q])
            ref = own_slab(p, 1, q, (pass_up[p].at[q],))
            send(ref, end_up[p].at[q], pes.at[p, q], per.at[p, q], up[p])
            arrived(pass_down[p].at[q], pas.at[p, 2 + q], par.at[p, 2 + q])
            ref = own_slab(p, 3, q + 2, (pass_down[p].at[q],))
            send(ref, end_down[p].at[q + 2], pes.at[p, 6 + q], per.at[p, 6 + q], down[p])
    for q in range(4):
        for p in parts:
            arrived(end_up[p].at[q], pes.at[p, q], per.at[p, q])
            arrived(end_down[p].at[q], pes.at[p, 4 + q], per.at[p, 4 + q])
            spread(
                p, at[ORDER[p][0]], middle_at(p, q), mid[p].at[q], (end_up[p].at[q], end_down[p].at[q])
            )
            if q < 3:
                send(mid[p].at[q], mid_in[p].at[q], bs.at[p, q], br.at[p, q], device(ORDER[p][1], away[q]))
    for p in parts:
        for q in range(3):
            arrived(mid_in[p].at[q], bs.at[p, q], br.at[p, q])
        total = mid[p][3].astype(F32)
        for q in range(3):
            total = total + mid_in[p][q].astype(F32)
        last[p][...] = total.astype(BF16)
        for q in range(3):
            place = (at[ORDER[p][2]] + away[q]) % SIDE
            send(last[p].at[place], last_in[p].at[q], cs.at[p, q], cr.at[p, q], device(ORDER[p][2], away[q]))
    results = []
    for p in parts:
        for q in range(3):
            arrived(last_in[p].at[q], cs.at[p, q], cr.at[p, q])
        total = last[p][at[ORDER[p][2]]].astype(F32)
        for q in range(3):
            total = total + last_in[p][q].astype(F32)
        results.append(total)
    for which in range(2):
        block = jnp.concatenate(
            [results[p][which * ROWS[p] : (which + 1) * ROWS[p]] for p in parts], axis=0
        )
        grad_ref[pl.ds(which * TILE, TILE), :] = block.T
    weight_grad_ref[:, pl.ds(0, TILE)] = results[2][64:65]
    weight_grad_ref[:, pl.ds(TILE, TILE)] = results[2][65:66]
    act_copy.wait()
    for copy in sends:
        copy.wait_send()


FORWARD_UNROLL = 4
TERM_UNROLL = 4


def on_device(features, weight, tile_values, tile_cols, tile_counts, cotangent):
    def vmem(*shape, dtype=BF16):
        return pltpu.VMEM(shape, dtype)

    def three(*lead, rows):
        return [vmem(*lead, rows[p], TILE) for p in range(3)]

    dma = pltpu.SemaphoreType.DMA
    anywhere, in_vmem = pl.BlockSpec(memory_space=pl.ANY), pl.BlockSpec(memory_space=pltpu.VMEM)
    scratch = (
        [vmem(129 * 16, UNIT, FIN), vmem(FIN, HID), vmem(2, SLOTS, TILE, TILE), vmem(256, HID)]
        + [vmem(2, SLOTS, dtype=I32)] * 2
        + [pltpu.SMEM((2, SLOTS), I32)] * 2
        + [vmem(256, HID)]
        + [vmem(4, 2, SLOTS, dtype=I32), pltpu.SMEM((4, 2, SLOTS), I32)]
        + [vmem(2, 8, TILE, dtype=I32)] * 3
        + [pltpu.SMEM((4, 8, TILE), I32)]
        + three(NONE + 1, rows=ROWS)
        + three(CHUNKS, rows=CHUNK)
        + three(2, 4, rows=CHUNK)
        + three(2, 4, rows=CHUNK)
        + three(4, 4, rows=CHUNK)
        + three(4, 4, rows=CHUNK)
        + three(4, 4, rows=CHUNK)
        + three(3, 4, rows=CHUNK)
        + three(4, rows=CHUNK)
        + three(3, rows=CHUNK)
        + [vmem(2 * FIN, TILE, dtype=F32)] * 2
        + [dma((13,)), dma, dma((3,))]
        + [dma((3, 3)), dma((3, 3)), dma((3, 12)), dma((3, 12)), dma((3, 8)), dma((3, 8))]
        + [dma((3, 12)), dma((3, 12)), dma((3, 16)), dma((3,))]
        + [dma((3, 4)), dma((3, 4)), dma((2,)), dma((2,)), dma((3, 4)), dma((3, 4)), dma((3, 8)), dma((3, 8))]
        + [dma((3, 3)), dma((3, 3)), dma((3, 3)), dma((3, 3))]
    )
    return pl.pallas_call(
        kernel,
        out_shape=(
            jax.ShapeDtypeStruct((256, HID), BF16),
            jax.ShapeDtypeStruct((256, FIN), F32),
            jax.ShapeDtypeStruct((1, HID), F32),
        ),
        in_specs=[anywhere] * 6,
        out_specs=(anywhere, in_vmem, in_vmem),
        scratch_shapes=scratch,
        compiler_params=pltpu.CompilerParams(
            collective_id=0, has_side_effects=True, vmem_limit_bytes=56 << 20
        ),
        name="graph_layer",
    )(features.reshape(16, UNIT, FIN), weight, tile_values, tile_cols, tile_counts, cotangent)


def solution(mesh):
    return jax.shard_map(
        on_device,
        mesh=mesh,
        in_specs=(
            P("dev", None),
            P(),
            P("dev", None, None, None),
            P("dev", None),
            P("dev", None),
            P("dev", None),
        ),
        out_specs=(P("dev", None), P("dev", None), P("dev", None)),
        check_vma=False,
    )
```

time: 907 us -> 72.8 us (0.08)
  waiting for transfers between devices: 848 us -> 0 us
  Pallas kernels: 0 us -> 67.7 us
  local copies, waits for them, and re-layouts: 22 us -> 4.37 us
  other arithmetic: 17 us -> 0 us
  between operations: 13.8 us -> 0.64 us
    reduce_scatter x1 -> x0, waiting for transfers between devices: 666 us -> none  [on_device(): lax.psum_scatter(column_terms, 'dev', scatter_dimension=0, tiled=True)]
    psum x1 -> x0, waiting for transfers between devices: 107 us -> none  [on_device(): weight_total = lax.psum(local_weight, 'dev')]
    all_gather x1 -> x0, waiting for transfers between devices: 73.4 us -> none  [on_device(): gathered = lax.all_gather(features, 'dev', axis=0, tiled=True)]
    pallas_call x0 -> x1, Pallas kernels: none -> 67.7 us  [on_device(): pl.pallas_call(kernel, out_shape=(jax.ShapeDtypeStruct((256, HID), BF16),...]
    scatter-add x1 -> x0, other arithmetic: 13.7 us -> none  [on_device(): jax.ops.segment_sum(widened.reshape(-1, tile_size, in_width), tile_cols.r...]
  transfers between devices with their start and end apart: 3 -> 0, of which waited for: 3 -> 0; matrix products, arithmetic and copies ran while one was open for 4% -> 0% of each run, Pallas kernels for 0% -> 0%
where the time goes in v2:
time: 72.8 us; the launch traced here: 72.7 us
  Pallas kernels  67.7 us (93%)
  local copies, waits for them, and re-layouts  4.37 us (6%)
    pallas_call x1, Pallas kernels, on_device(): pl.pallas_call(kernel, out_shape=(jax.ShapeDtypeStruct((256, HID), BF16),...  67.7 us
    unnamed x3, local copies, waits for them, and re-layouts  4.37 us

profile of v2, /device:TPU:0, one launch (start us, length us, event | category | flops | bytes accessed | tf_op | source)
XLA Modules:
  0.0 72.7 jit_solution(11636673423476190257)
XLA Ops:
  0.6 67.7 %graph_layer.1 = (bf16[256,256]{1,0:T(8,128)(2,1)}, f32[256,128]{1,0:T(8,128)}, f32[1,256]{1,0:T(1,128)}) custom-call(bf16[16,16,128]{2,1,0:T(8,128)(2,1)} %bitcast.1, bf16[128,256]{1,0:T(8,128)(2,1)} %weight_hbm.1, bf16[2,32,128,128]{3,2,1,0:T(8,128)(2,1)} %tiles_hbm.1, s32[2,32]{1,0:T(2,128)} %cols_hbm.1, s32[2,32]{1,0:T(2,128)} %counts_hbm.1, ...), custom_call_target="tpu_custom_call" | custom-call | tf_op jit(solution)/shard_map/graph_layer/pallas_call | solution.py:442
  68.3 1.6 %copy.12 = bf16[256,256]{1,0:T(8,128)(2,1)} copy(bf16[256,256]{1,0:T(8,128)(2,1)} %get-tuple-element.6) | data formatting | bytes 262144
  69.9 1.6 %copy.13 = f32[256,128]{1,0:T(8,128)} copy(f32[256,128]{1,0:T(8,128)} %get-tuple-element.7) | data formatting | bytes 262144
  71.4 1.2 %copy.14 = f32[1,256]{1,0:T(1,128)} copy(f32[1,256]{1,0:T(1,128)} %get-tuple-element.8) | data formatting | bytes 2048

commit v3 on v2

--- a/solution.py
+++ b/solution.py
@@ -28,19 +28,18 @@
 
 def kernel(
     features_hbm, weight_hbm, tiles_hbm, cols_hbm, counts_hbm, cotangent_hbm,
-    act_hbm, grad_ref, weight_grad_ref,
-    gathered, w_ref, tiles, ct_ref, cols_ref, counts_ref, cols_smem, counts_smem, act_ref,
+    act_ref, grad_ref, weight_grad_ref,
+    gathered, w_ref, tiles, ct_ref, cols_ref, counts_ref, cols_smem, counts_smem,
     place_ref, place_smem, slot_ref, twin_slot_out, twin_slot_ref, slot_smem, t0, t1, t2, own0, own1, own2,
     pass_up0, pass_up1, pass_up2, pass_down0, pass_down1, pass_down2,
-    end_up0, end_up1, end_up2, end_down0, end_down1, end_down2,
+    end0, end1, end2,
     b0, b1, b2, rb0, rb1, rb2, c0, c1, c2, rc0, rc1, rc2, wg_ref, twin_wg_ref,
-    load_sem, act_sem, table_sem, g1s, g1r, g2s, g2r, gos, gor, g3s, g3r, gcs, gcr, ts, tr, es, er,
-    pas, par, pes, per, bs, br, cs, cr,
+    load_sem, table_sem, gs, g1r, g2r, gor, g3r, gcr, ts, tr, es, er, rs, par, per, br, cr,
 ):
     parts = range(3)
     terms, own = (t0, t1, t2), (own0, own1, own2)
     pass_up, pass_down = (pass_up0, pass_up1, pass_up2), (pass_down0, pass_down1, pass_down2)
-    end_up, end_down = (end_up0, end_up1, end_up2), (end_down0, end_down1, end_down2)
+    end = (end0, end1, end2)
     mid, mid_in = (b0, b1, b2), (rb0, rb1, rb2)
     last, last_in = (c0, c1, c2), (rc0, rc1, rc2)
 
@@ -73,85 +72,80 @@
 
     loads = []
 
-    def load(src, dst):
-        copy = pltpu.make_async_copy(src, dst, load_sem.at[len(loads)])
+    def load(src, dst, n):
+        copy = pltpu.make_async_copy(src, dst, load_sem.at[n])
         copy.start()
         loads.append(copy)
 
     for p, first, unit, count in ((0, 0, 0, 3), (1, 3, 0, 3), (2, 6, 0, 2), (0, 8, 3, 3), (1, 11, 3, 2), (2, 13, 2, 3)):
         place = BASE[p] + (core * CHUNKS + (i3[p] * SIDE + i2[p]) * SIDE + i1[p]) * UNITS[p] + unit
-        load(features_hbm.at[pl.ds(first, count)], gathered.at[pl.ds(place, count)])
-    load(cols_hbm, cols_smem)
-    load(counts_hbm, counts_smem)
-    load(cols_hbm, cols_ref)
-    load(counts_hbm, counts_ref)
-    load(tiles_hbm, tiles)
-    load(weight_hbm, w_ref)
-    load(cotangent_hbm, ct_ref)
-
-    sends = []
+        load(features_hbm.at[pl.ds(first, count)], gathered.at[pl.ds(place, count)], 0)
+    load(cols_hbm, cols_smem, 1)
+    load(counts_hbm, counts_smem, 2)
+    load(cols_hbm, cols_ref, 3)
+    load(counts_hbm, counts_ref, 4)
+    load(tiles_hbm, tiles, 5)
+    load(weight_hbm, w_ref, 6)
+    load(cotangent_hbm, ct_ref, 7)
 
     def send(src, dst, ssem, rsem, to):
         copy = pltpu.make_async_remote_copy(
             src_ref=src, dst_ref=dst, send_sem=ssem, recv_sem=rsem, device_id=to, device_id_type=MESH
         )
         copy.start()
-        sends.append(copy)
-
-    def arrived(dst, ssem, rsem):
+
+    def arrived(dst, rsem):
         pltpu.make_async_remote_copy(
-            src_ref=dst, dst_ref=dst, send_sem=ssem, recv_sem=rsem, device_id=twin, device_id_type=MESH
+            src_ref=dst, dst_ref=dst, send_sem=es.at[0], recv_sem=rsem, device_id=twin, device_id_type=MESH
         ).wait_recv()
 
-    for copy in loads[:6]:
-        copy.wait()
+    def sent(src, ssem):
+        pltpu.make_async_remote_copy(
+            src_ref=src, dst_ref=src, send_sem=ssem, recv_sem=er.at[0], device_id=twin, device_id_type=MESH
+        ).wait_send()
+
+    pltpu.make_async_copy(features_hbm, gathered.at[pl.ds(0, 16)], load_sem.at[0]).wait()
     pl.semaphore_wait(barrier, 10)
 
     def first_sends(p, r):
         fast = i1[p] if r == 0 else (i1[p] + SIDE - HOPS[r - 1]) % SIDE
         ref = chunk(p, i3[p], i2[p], fast)
         if r > 0:
-            arrived(ref, g1s.at[p, r - 1], g1r.at[p, r - 1])
+            arrived(ref, g1r.at[p, r - 1])
         for n, hop in enumerate(HOPS):
-            send(ref, ref, g2s.at[p, r * 3 + n], g2r.at[p, r * 3 + n], move(i2[p], s2[p], hop))
+            send(ref, ref, gs.at[p], g2r.at[p, n], move(i2[p], s2[p], hop))
         return ref
 
     for p in parts:
         mine = chunk(p, i3[p], i2[p], i1[p])
         for n, hop in enumerate(HOPS):
-            send(mine, mine, g1s.at[p, n], g1r.at[p, n], move(i1[p], s1[p], hop))
+            send(mine, mine, gs.at[p], g1r.at[p, n], move(i1[p], s1[p], hop))
     for r in range(4):
         refs = [first_sends(p, r) for p in parts]
         for p in parts:
             for n, hop in enumerate((1, 3)):
-                k = r * 2 + n
-                send(refs[p], refs[p], gos.at[p, k], gor.at[p, k], move(i3[p], s3[p], hop))
+                send(refs[p], refs[p], gs.at[p], gor.at[p, n], move(i3[p], s3[p], hop))
 
     def slab(p, slow, r):
         middle = i2[p] if r == 0 else (i2[p] + SIDE - HOPS[r - 1]) % SIDE
         return chunk(p, slow, middle, 0, SIDE)
 
     def to_the_twin(p, ref, n):
-        send(ref, ref, gcs.at[p, n], gcr.at[p], twin)
+        send(ref, ref, gs.at[p], gcr.at[p], twin)
 
     def slab_arrived(p, r, slow, n):
         ref = slab(p, slow, r)
-        if r == 0:
-            for s in range(4):
-                fast = i1[p] if s == 0 else (i1[p] + SIDE - HOPS[s - 1]) % SIDE
-                arrived(chunk(p, slow, i2[p], fast), gos.at[p, s * 2 + n], gor.at[p, s * 2 + n])
-        else:
-            arrived(ref, g3s.at[p, 2 * r + n], g3r.at[p, 2 * r + n])
+        arrived(ref, gor.at[p, n] if r == 0 else g3r.at[p, 2 * (r - 1) + n])
         return ref
 
     def pass_on(p, r):
         up = slab_arrived(p, r, (i3[p] + 3) % SIDE, 0)
         if r < 2:
-            send(up, up, g3s.at[p, 8 + r], g3r.at[p, 8 + r], move(i3[p], s3[p], 1))
+            send(up, up, gs.at[p], g3r.at[p, 6 + r], move(i3[p], s3[p], 1))
         to_the_twin(p, up, 4 + 2 * r)
         down = slab_arrived(p, r, (i3[p] + 1) % SIDE, 1)
         if r >= 2:
-            send(down, down, g3s.at[p, 8 + r], g3r.at[p, 8 + r], move(i3[p], s3[p], 3))
+            send(down, down, gs.at[p], g3r.at[p, 6 + r], move(i3[p], s3[p], 3))
         to_the_twin(p, down, 5 + 2 * r)
 
     for p in parts:
@@ -202,13 +196,9 @@
     for r in range(1, 4):
         for p in parts:
             ref = slab(p, i3[p], r)
-            middle = (i2[p] + SIDE - HOPS[r - 1]) % SIDE
-            for s in range(4):
-                fast = i1[p] if s == 0 else (i1[p] + SIDE - HOPS[s - 1]) % SIDE
-                n = s * 3 + r - 1
-                arrived(chunk(p, i3[p], middle, fast), g2s.at[p, n], g2r.at[p, n])
-            send(ref, ref, g3s.at[p, 2 * r], g3r.at[p, 2 * r], move(i3[p], s3[p], 1))
-            send(ref, ref, g3s.at[p, 2 * r + 1], g3r.at[p, 2 * r + 1], move(i3[p], s3[p], 3))
+            arrived(ref, g2r.at[p, r - 1])
+            send(ref, ref, gs.at[p], g3r.at[p, 2 * r - 2], move(i3[p], s3[p], 1))
+            send(ref, ref, gs.at[p], g3r.at[p, 2 * r - 1], move(i3[p], s3[p], 3))
             to_the_twin(p, ref, r)
         for p in parts:
             pass_on(p, r - 1)
@@ -217,16 +207,16 @@
     for r in range(4):
         for p in parts:
             ref = slab(p, (i3[p] + 2) % SIDE, r)
-            arrived(ref, g3s.at[p, 8 + r], g3r.at[p, 8 + r])
+            arrived(ref, g3r.at[p, 6 + r])
             to_the_twin(p, ref, 12 + r)
     place_copy.wait()
     slot_copy.wait()
-    arrived(twin_slot_ref, es.at[0], er.at[0])
+    arrived(twin_slot_ref, er.at[0])
     twin_slot_copy = pltpu.make_async_copy(twin_slot_ref, slot_smem.at[pl.ds(2, 2)], table_sem.at[2])
     twin_slot_copy.start()
     for p in parts:
         arrived(
-            gathered.at[pl.ds(BASE[p] + (1 - core) * CHUNKS * UNITS[p], CHUNKS * UNITS[p])], gcs.at[p, 0], gcr.at[p]
+            gathered.at[pl.ds(BASE[p] + (1 - core) * CHUNKS * UNITS[p], CHUNKS * UNITS[p])], gcr.at[p]
         )
 
     def block_of(b, slot):
@@ -257,8 +247,6 @@
     pre = jnp.dot(aggregated, weight, preferred_element_type=F32)
     sigma = jax.nn.sigmoid(pre)
     act_ref[...] = (pre * sigma).astype(BF16)
-    act_copy = pltpu.make_async_copy(act_ref, act_hbm, act_sem)
-    act_copy.start()
     delta = (ct_ref[...].astype(F32) * sigma * (1.0 + pre * (1.0 - sigma))).astype(BF16)
     back = lax.dot_general(
         weight, delta, (((1,), (1,)), ((), ())), preferred_element_type=F32
@@ -282,10 +270,9 @@
             lax.fori_loop(0, 8 // TERM_UNROLL, term_step, 0)
             for p in parts:
                 first = b * SLOTS + group * 16
-                n = b * 2 + group
                 send(
                     terms[p].at[pl.ds(first, 16)], terms[p].at[pl.ds(2 * SLOTS + first, 16)],
-                    ts.at[p, n], tr.at[p, n], twin,
+                    ts.at[p], tr.at[p], twin,
                 )
     weight_terms = lax.dot_general(
         aggregated, delta, (((0,), (0,)), ((), ())), preferred_element_type=F32
@@ -295,9 +282,8 @@
     send(wg_ref, twin_wg_ref, es.at[1], er.at[1], twin)
     twin_slot_copy.wait()
     for p in parts:
-        for n in range(4):
-            arrived(terms[p].at[pl.ds(2 * SLOTS + n * 16, 16)], ts.at[p, n], tr.at[p, n])
-    arrived(twin_wg_ref, es.at[1], er.at[1])
+        arrived(terms[p].at[pl.ds(2 * SLOTS, 2 * SLOTS)], tr.at[p])
+    arrived(twin_wg_ref, er.at[1])
 
     row = lax.broadcasted_iota(I32, (EXTRA, TILE), 0)
 
@@ -347,44 +333,39 @@
         for p in parts:
             ref = own_slab(p, 2, q)
             if q < 2:
-                send(ref, pass_up[p].at[q], pas.at[p, q], par.at[p, q], up[p])
+                send(ref, pass_up[p].at[q], rs.at[p], par.at[p, q], up[p])
             else:
-                send(ref, pass_down[p].at[q - 2], pas.at[p, q], par.at[p, q], down[p])
+                send(ref, pass_down[p].at[q - 2], rs.at[p], par.at[p, q], down[p])
     for q in range(2):
         for p in parts:
-            send(own_slab(p, 1, q + 2), end_up[p].at[q + 2], pes.at[p, q + 2], per.at[p, q + 2], up[p])
-            send(own_slab(p, 3, q), end_down[p].at[q], pes.at[p, 4 + q], per.at[p, 4 + q], down[p])
+            send(own_slab(p, 1, q + 2), end[p].at[q + 2, 0], rs.at[p], per.at[p, q + 2], up[p])
+            send(own_slab(p, 3, q), end[p].at[q, 1], rs.at[p], per.at[p, q], down[p])
     for q in range(2):
         for p in parts:
-            arrived(pass_up[p].at[q], pas.at[p, q], par.at[p, q])
+            arrived(pass_up[p].at[q], par.at[p, q])
             ref = own_slab(p, 1, q, (pass_up[p].at[q],))
-            send(ref, end_up[p].at[q], pes.at[p, q], per.at[p, q], up[p])
-            arrived(pass_down[p].at[q], pas.at[p, 2 + q], par.at[p, 2 + q])
+            send(ref, end[p].at[q, 0], rs.at[p], per.at[p, q], up[p])
+            arrived(pass_down[p].at[q], par.at[p, 2 + q])
             ref = own_slab(p, 3, q + 2, (pass_down[p].at[q],))
-            send(ref, end_down[p].at[q + 2], pes.at[p, 6 + q], per.at[p, 6 + q], down[p])
+            send(ref, end[p].at[q + 2, 1], rs.at[p], per.at[p, q + 2], down[p])
     for q in range(4):
         for p in parts:
-            arrived(end_up[p].at[q], pes.at[p, q], per.at[p, q])
-            arrived(end_down[p].at[q], pes.at[p, 4 + q], per.at[p, 4 + q])
-            spread(
-                p, at[ORDER[p][0]], middle_at(p, q), mid[p].at[q], (end_up[p].at[q], end_down[p].at[q])
-            )
+            arrived(end[p].at[q], per.at[p, q])
+            spread(p, at[ORDER[p][0]], middle_at(p, q), mid[p].at[q], (end[p].at[q, 0], end[p].at[q, 1]))
             if q < 3:
-                send(mid[p].at[q], mid_in[p].at[q], bs.at[p, q], br.at[p, q], device(ORDER[p][1], away[q]))
-    for p in parts:
-        for q in range(3):
-            arrived(mid_in[p].at[q], bs.at[p, q], br.at[p, q])
+                send(mid[p].at[q], mid_in[p].at[q], rs.at[p], br.at[p], device(ORDER[p][1], away[q]))
+    for p in parts:
+        arrived(mid_in[p], br.at[p])
         total = mid[p][3].astype(F32)
         for q in range(3):
             total = total + mid_in[p][q].astype(F32)
         last[p][...] = total.astype(BF16)
         for q in range(3):
             place = (at[ORDER[p][2]] + away[q]) % SIDE
-            send(last[p].at[place], last_in[p].at[q], cs.at[p, q], cr.at[p, q], device(ORDER[p][2], away[q]))
+            send(last[p].at[place], last_in[p].at[q], rs.at[p], cr.at[p], device(ORDER[p][2], away[q]))
     results = []
     for p in parts:
-        for q in range(3):
-            arrived(last_in[p].at[q], cs.at[p, q], cr.at[p, q])
+        arrived(last_in[p], cr.at[p])
         total = last[p][at[ORDER[p][2]]].astype(F32)
         for q in range(3):
             total = total + last_in[p][q].astype(F32)
@@ -396,9 +377,18 @@
         grad_ref[pl.ds(which * TILE, TILE), :] = block.T
     weight_grad_ref[:, pl.ds(0, TILE)] = results[2][64:65]
     weight_grad_ref[:, pl.ds(TILE, TILE)] = results[2][65:66]
-    act_copy.wait()
-    for copy in sends:
-        copy.wait_send()
+    for p in parts:
+        sent(gathered.at[pl.ds(BASE[p], 127 * UNITS[p])], gs.at[p])
+        sent(terms[p].at[pl.ds(0, 2 * SLOTS)], ts.at[p])
+        sent(own[p].at[pl.ds(0, 63)], rs.at[p])
+    sent(twin_slot_out, es.at[0])
+    sent(wg_ref, es.at[1])
+
+
+def hand_over(act_in, grad_in, weight_grad_in, act_ref, grad_ref, weight_grad_ref):
+    act_ref[...] = act_in[...]
+    grad_ref[...] = grad_in[...]
+    weight_grad_ref[...] = weight_grad_in[...]
 
 
 FORWARD_UNROLL = 4
@@ -413,12 +403,11 @@
         return [vmem(*lead, rows[p], TILE) for p in range(3)]
 
     dma = pltpu.SemaphoreType.DMA
-    anywhere, in_vmem = pl.BlockSpec(memory_space=pl.ANY), pl.BlockSpec(memory_space=pltpu.VMEM)
+    in_hbm, in_vmem = pl.BlockSpec(memory_space=pltpu.HBM), pl.BlockSpec(memory_space=pltpu.VMEM)
     scratch = (
         [vmem(129 * 16, UNIT, FIN), vmem(FIN, HID), vmem(2, SLOTS, TILE, TILE), vmem(256, HID)]
         + [vmem(2, SLOTS, dtype=I32)] * 2
         + [pltpu.SMEM((2, SLOTS), I32)] * 2
-        + [vmem(256, HID)]
         + [vmem(4, 2, SLOTS, dtype=I32), pltpu.SMEM((4, 2, SLOTS), I32)]
         + [vmem(2, 8, TILE, dtype=I32)] * 3
         + [pltpu.SMEM((4, 8, TILE), I32)]
@@ -426,34 +415,42 @@
         + three(CHUNKS, rows=CHUNK)
         + three(2, 4, rows=CHUNK)
         + three(2, 4, rows=CHUNK)
-        + three(4, 4, rows=CHUNK)
-        + three(4, 4, rows=CHUNK)
+        + three(4, 2, 4, rows=CHUNK)
         + three(4, 4, rows=CHUNK)
         + three(3, 4, rows=CHUNK)
         + three(4, rows=CHUNK)
         + three(3, rows=CHUNK)
         + [vmem(2 * FIN, TILE, dtype=F32)] * 2
-        + [dma((13,)), dma, dma((3,))]
-        + [dma((3, 3)), dma((3, 3)), dma((3, 12)), dma((3, 12)), dma((3, 8)), dma((3, 8))]
-        + [dma((3, 12)), dma((3, 12)), dma((3, 16)), dma((3,))]
-        + [dma((3, 4)), dma((3, 4)), dma((2,)), dma((2,)), dma((3, 4)), dma((3, 4)), dma((3, 8)), dma((3, 8))]
-        + [dma((3, 3)), dma((3, 3)), dma((3, 3)), dma((3, 3))]
+        + [dma((8,)), dma((3,)), dma((3,)), dma((3, 3)), dma((3, 3)), dma((3, 2)), dma((3, 10)), dma((3,))]
+        + [dma((3,)), dma((3,)), dma((2,)), dma((2,)), dma((3,)), dma((3, 4)), dma((3, 4)), dma((3,)), dma((3,))]
     )
-    return pl.pallas_call(
+    shapes = (
+        jax.ShapeDtypeStruct((256, HID), BF16),
+        jax.ShapeDtypeStruct((256, FIN), F32),
+        jax.ShapeDtypeStruct((1, HID), F32),
+    )
+    results = pl.pallas_call(
         kernel,
-        out_shape=(
-            jax.ShapeDtypeStruct((256, HID), BF16),
-            jax.ShapeDtypeStruct((256, FIN), F32),
-            jax.ShapeDtypeStruct((1, HID), F32),
-        ),
-        in_specs=[anywhere] * 6,
-        out_specs=(anywhere, in_vmem, in_vmem),
+        out_shape=shapes,
+        in_specs=[in_hbm] * 6,
+        out_specs=(in_vmem,) * 3,
         scratch_shapes=scratch,
         compiler_params=pltpu.CompilerParams(
-            collective_id=0, has_side_effects=True, vmem_limit_bytes=56 << 20
+            collective_id=0, has_side_effects=True, vmem_limit_bytes=48 << 20
         ),
         name="graph_layer",
-    )(features.reshape(16, UNIT, FIN), weight, tile_values, tile_cols, tile_counts, cotangent)
+    )(*(
+        pltpu.with_memory_space_constraint(x, pltpu.HBM)
+        for x in (features.reshape(16, UNIT, FIN), weight, tile_values, tile_cols, tile_counts, cotangent)
+    ))
+    return pl.pallas_call(
+        hand_over,
+        out_shape=shapes,
+        in_specs=[in_vmem] * 3,
+        out_specs=(in_vmem,) * 3,
+        compiler_params=pltpu.CompilerParams(vmem_limit_bytes=4 << 20),
+        name="hand_over",
+    )(*results)
 
 
 def solution(mesh):

time: 72.8 us -> 65.4 us (0.90)
  local copies, waits for them, and re-layouts: 4.37 us -> 0 us
  Pallas kernels: 67.7 us -> 64.7 us
    unnamed x3 -> x0, local copies, waits for them, and re-layouts: 4.37 us -> none
    pallas_call x1 -> x2, Pallas kernels: 67.7 us -> 64.7 us  [the longest x1 64 us: on_device(): pl.pallas_call(kernel, out_shape=shapes, in_specs=[in_hbm] * 6, out_specs...]
where the time goes in v3:
time: 65.4 us; the launch traced here: 65.3 us
  Pallas kernels  64.7 us (99%)
    pallas_call x1, Pallas kernels, on_device(): pl.pallas_call(kernel, out_shape=shapes, in_specs=[in_hbm] * 6, out_specs...  64 us

profile of v3, /device:TPU:0, one launch (start us, length us, event | category | flops | bytes accessed | tf_op | source)
XLA Modules:
  0.0 65.3 jit_solution(9866518785728153889)
XLA Ops:
  0.6 64.0 %graph_layer.1 = (bf16[256,256]{1,0:T(8,128)(2,1)S(1)}, f32[256,128]{1,0:T(8,128)S(1)}, f32[1,256]{1,0:T(1,128)S(1)}) custom-call(bf16[16,16,128]{2,1,0:T(8,128)(2,1)} %bitcast.1, bf16[128,256]{1,0:T(8,128)(2,1)} %weight_hbm.1, bf16[2,32,128,128]{3,2,1,0:T(8,128)(2,1)} %tiles_hbm.1, s32[2,32]{1,0:T(2,128)} %cols_hbm.1, s32[2,32]{1,0:T(2,128)} %counts_hbm.1, ...), custom_call_target="tpu_custom_call" | custom-call | tf_op jit(solution)/shard_map/graph_layer/pallas_call | solution.py:432
  64.6 0.7 %hand_over.1 = (bf16[256,256]{1,0:T(8,128)(2,1)}, f32[256,128]{1,0:T(8,128)}, f32[1,256]{1,0:T(1,128)}) custom-call(bf16[256,256]{1,0:T(8,128)(2,1)S(1)} %get-tuple-element.6.act_in, f32[256,128]{1,0:T(8,128)S(1)} %get-tuple-element.7.grad_in, f32[1,256]{1,0:T(1,128)S(1)} %get-tuple-element.8.weight_grad_in), custom_call_target="tpu_custom_call" | custom-call | tf_op jit(solution)/shard_map/hand_over/pallas_call | solution.py:446

commit v4 on v3

--- a/solution.py
+++ b/solution.py
@@ -34,7 +34,7 @@
     pass_up0, pass_up1, pass_up2, pass_down0, pass_down1, pass_down2,
     end0, end1, end2,
     b0, b1, b2, rb0, rb1, rb2, c0, c1, c2, rc0, rc1, rc2, wg_ref, twin_wg_ref,
-    load_sem, table_sem, gs, g1r, g2r, gor, g3r, gcr, ts, tr, es, er, rs, par, per, br, cr,
+    load_sem, table_sem, gs, g1r, g2r, g3r, gfr, gcr, ts, tr, es, er, rs, par, per, br, cr,
 ):
     parts = range(3)
     terms, own = (t0, t1, t2), (own0, own1, own2)
@@ -66,8 +66,8 @@
     def move(index, stride, hop):
         return (me + ((index + hop) % SIDE - index) * stride,)
 
-    def chunk(p, slow, middle, fast, count=1):
-        at_chunk = core * CHUNKS + (slow * SIDE + middle) * SIDE + fast
+    def chunk(p, slow, fast, middle, count=1):
+        at_chunk = core * CHUNKS + (slow * SIDE + fast) * SIDE + middle
         return gathered.at[pl.ds(BASE[p] + at_chunk * UNITS[p], count * UNITS[p])]
 
     loads = []
@@ -78,7 +78,7 @@
         loads.append(copy)
 
     for p, first, unit, count in ((0, 0, 0, 3), (1, 3, 0, 3), (2, 6, 0, 2), (0, 8, 3, 3), (1, 11, 3, 2), (2, 13, 2, 3)):
-        place = BASE[p] + (core * CHUNKS + (i3[p] * SIDE + i2[p]) * SIDE + i1[p]) * UNITS[p] + unit
+        place = BASE[p] + (core * CHUNKS + (i3[p] * SIDE + i1[p]) * SIDE + i2[p]) * UNITS[p] + unit
         load(features_hbm.at[pl.ds(first, count)], gathered.at[pl.ds(place, count)], 0)
     load(cols_hbm, cols_smem, 1)
     load(counts_hbm, counts_smem, 2)
@@ -107,50 +107,61 @@
     pltpu.make_async_copy(features_hbm, gathered.at[pl.ds(0, 16)], load_sem.at[0]).wait()
     pl.semaphore_wait(barrier, 10)
 
+    def fast_at(p, r):
+        return i1[p] if r == 0 else (i1[p] + SIDE - HOPS[r - 1]) % SIDE
+
+    def along_third(p, r, ref):
+        for n, hop in enumerate((1, 3)):
+            send(ref, ref, gs.at[p], g3r.at[p, 2 * r + n], move(i3[p], s3[p], hop))
+
     def first_sends(p, r):
-        fast = i1[p] if r == 0 else (i1[p] + SIDE - HOPS[r - 1]) % SIDE
-        ref = chunk(p, i3[p], i2[p], fast)
+        ref = chunk(p, i3[p], fast_at(p, r), i2[p])
         if r > 0:
             arrived(ref, g1r.at[p, r - 1])
         for n, hop in enumerate(HOPS):
-            send(ref, ref, gs.at[p], g2r.at[p, n], move(i2[p], s2[p], hop))
+            send(ref, ref, gs.at[p], g2r.at[p, r * 3 + n], move(i2[p], s2[p], hop))
         return ref
 
     for p in parts:
-        mine = chunk(p, i3[p], i2[p], i1[p])
+        mine = chunk(p, i3[p], i1[p], i2[p])
         for n, hop in enumerate(HOPS):
             send(mine, mine, gs.at[p], g1r.at[p, n], move(i1[p], s1[p], hop))
     for r in range(4):
         refs = [first_sends(p, r) for p in parts]
         for p in parts:
-            for n, hop in enumerate((1, 3)):
-                send(refs[p], refs[p], gs.at[p], gor.at[p, n], move(i3[p], s3[p], hop))
-
-    def slab(p, slow, r):
-        middle = i2[p] if r == 0 else (i2[p] + SIDE - HOPS[r - 1]) % SIDE
-        return chunk(p, slow, middle, 0, SIDE)
-
-    def to_the_twin(p, ref, n):
+            along_third(p, r, refs[p])
+
+    def group(p, slow, r, first=0, count=SIDE):
+        return chunk(p, slow, fast_at(p, r), first, count)
+
+    def to_the_twin(p, ref):
         send(ref, ref, gs.at[p], gcr.at[p], twin)
 
-    def slab_arrived(p, r, slow, n):
-        ref = slab(p, slow, r)
-        arrived(ref, gor.at[p, n] if r == 0 else g3r.at[p, 2 * (r - 1) + n])
-        return ref
+    def last_sends(p, r):
+        for n, hop in enumerate(HOPS):
+            ref = chunk(p, i3[p], fast_at(p, r), (i2[p] + SIDE - hop) % SIDE)
+            arrived(ref, g2r.at[p, r * 3 + n])
+            along_third(p, r, ref)
+        to_the_twin(p, group(p, i3[p], r))
 
     def pass_on(p, r):
-        up = slab_arrived(p, r, (i3[p] + 3) % SIDE, 0)
-        if r < 2:
-            send(up, up, gs.at[p], g3r.at[p, 6 + r], move(i3[p], s3[p], 1))
-        to_the_twin(p, up, 4 + 2 * r)
-        down = slab_arrived(p, r, (i3[p] + 1) % SIDE, 1)
-        if r >= 2:
-            send(down, down, gs.at[p], g3r.at[p, 6 + r], move(i3[p], s3[p], 3))
-        to_the_twin(p, down, 5 + 2 * r)
-
-    for p in parts:
-        to_the_twin(p, slab(p, i3[p], 0), 0)
-
+        below, above = (i3[p] + 3) % SIDE, (i3[p] + 1) % SIDE
+        arrived(group(p, below, r), g3r.at[p, 2 * r])
+        half = group(p, below, r, 0, 2)
+        send(half, half, gs.at[p], gfr.at[p, r], move(i3[p], s3[p], 1))
+        arrived(group(p, above, r), g3r.at[p, 2 * r + 1])
+        half = group(p, above, r, 2, 2)
+        send(half, half, gs.at[p], gfr.at[p, r], move(i3[p], s3[p], 3))
+        to_the_twin(p, group(p, below, r))
+        to_the_twin(p, group(p, above, r))
+
+    def opposite(p, r):
+        ref = group(p, (i3[p] + 2) % SIDE, r)
+        arrived(ref, gfr.at[p, r])
+        to_the_twin(p, ref)
+
+    for p in parts:
+        last_sends(p, 0)
     for p in parts:
         gathered[pl.ds(BASE[p] + 2 * CHUNKS * UNITS[p], UNITS[p])] = jnp.zeros((UNITS[p], UNIT, FIN), BF16)
         terms[p][NONE] = jnp.zeros((ROWS[p], TILE), BF16)
@@ -164,7 +175,7 @@
     for p in parts:
         turned = (col_core + p) % 3
         flat = col_core
-        for n in range(3):
+        for n in (0, 2, 1):
             flat = flat * SIDE + pick((turned + n) % 3, where)
         starts.append(BASE[p] + jnp.where(live, flat, 2 * CHUNKS) * UNITS[p])
     place_ref[0] = starts[0] + 3 * half
@@ -192,23 +203,24 @@
     send(twin_slot_out, twin_slot_ref, es.at[0], er.at[0], twin)
     slot_copy = pltpu.make_async_copy(slot_ref, slot_smem.at[pl.ds(0, 2)], table_sem.at[1])
     slot_copy.start()
-
-    for r in range(1, 4):
-        for p in parts:
-            ref = slab(p, i3[p], r)
-            arrived(ref, g2r.at[p, r - 1])
-            send(ref, ref, gs.at[p], g3r.at[p, 2 * r - 2], move(i3[p], s3[p], 1))
-            send(ref, ref, gs.at[p], g3r.at[p, 2 * r - 1], move(i3[p], s3[p], 3))
-            to_the_twin(p, ref, r)
-        for p in parts:
-            pass_on(p, r - 1)
-    for p in parts:
-        pass_on(p, 3)
-    for r in range(4):
-        for p in parts:
-            ref = slab(p, (i3[p] + 2) % SIDE, r)
-            arrived(ref, g3r.at[p, 6 + r])
-            to_the_twin(p, ref, 12 + r)
+    for p in parts:
+        last_sends(p, 1)
+    for p in parts:
+        pass_on(p, 0)
+    for p in parts:
+        last_sends(p, 2)
+    for p in parts:
+        pass_on(p, 1)
+    for p in parts:
+        last_sends(p, 3)
+    for r in range(2, 4):
+        for p in parts:
+            pass_on(p, r)
+        for p in parts:
+            opposite(p, r - 2)
+    for r in range(2, 4):
+        for p in parts:
+            opposite(p, r)
     place_copy.wait()
     slot_copy.wait()
     arrived(twin_slot_ref, er.at[0])
@@ -421,7 +433,7 @@
         + three(4, rows=CHUNK)
         + three(3, rows=CHUNK)
         + [vmem(2 * FIN, TILE, dtype=F32)] * 2
-        + [dma((8,)), dma((3,)), dma((3,)), dma((3, 3)), dma((3, 3)), dma((3, 2)), dma((3, 10)), dma((3,))]
+        + [dma((8,)), dma((3,)), dma((3,)), dma((3, 3)), dma((3, 12)), dma((3, 8)), dma((3, 4)), dma((3,))]
         + [dma((3,)), dma((3,)), dma((2,)), dma((2,)), dma((3,)), dma((3, 4)), dma((3, 4)), dma((3,)), dma((3,))]
     )
     shapes = (

time: 65.4 us -> 63.7 us (0.974)
  Pallas kernels: 64.7 us -> 62.9 us
    pallas_call x1, Pallas kernels: 64 us -> 62.2 us  [on_device(): pl.pallas_call(kernel, out_shape=shapes, in_specs=[in_hbm] * 6, out_specs...]
where the time goes in v4:
time: 63.7 us; the launch traced here: 63.5 us
  Pallas kernels  62.9 us (99%)
  between operations  0.64 us (1%)
    pallas_call x1, Pallas kernels, on_device(): pl.pallas_call(kernel, out_shape=shapes, in_specs=[in_hbm] * 6, out_specs...  62.2 us

profile of v4, /device:TPU:0, one launch (start us, length us, event | category | flops | bytes accessed | tf_op | source)
XLA Modules:
  0.0 63.5 jit_solution(11535650554374470044)
XLA Ops:
  0.6 62.2 %graph_layer.1 = (bf16[256,256]{1,0:T(8,128)(2,1)S(1)}, f32[256,128]{1,0:T(8,128)S(1)}, f32[1,256]{1,0:T(1,128)S(1)}) custom-call(bf16[16,16,128]{2,1,0:T(8,128)(2,1)} %bitcast.1, bf16[128,256]{1,0:T(8,128)(2,1)} %weight_hbm.1, bf16[2,32,128,128]{3,2,1,0:T(8,128)(2,1)} %tiles_hbm.1, s32[2,32]{1,0:T(2,128)} %cols_hbm.1, s32[2,32]{1,0:T(2,128)} %counts_hbm.1, ...), custom_call_target="tpu_custom_call" | custom-call | tf_op jit(solution)/shard_map/graph_layer/pallas_call | solution.py:444
  62.8 0.7 %hand_over.1 = (bf16[256,256]{1,0:T(8,128)(2,1)}, f32[256,128]{1,0:T(8,128)}, f32[1,256]{1,0:T(1,128)}) custom-call(bf16[256,256]{1,0:T(8,128)(2,1)S(1)} %get-tuple-element.6.act_in, f32[256,128]{1,0:T(8,128)S(1)} %get-tuple-element.7.grad_in, f32[1,256]{1,0:T(1,128)S(1)} %get-tuple-element.8.weight_grad_in), custom_call_target="tpu_custom_call" | custom-call | tf_op jit(solution)/shard_map/hand_over/pallas_call | solution.py:458

commit v5 on v4

--- a/solution.py
+++ b/solution.py
@@ -33,14 +33,14 @@
     place_ref, place_smem, slot_ref, twin_slot_out, twin_slot_ref, slot_smem, t0, t1, t2, own0, own1, own2,
     pass_up0, pass_up1, pass_up2, pass_down0, pass_down1, pass_down2,
     end0, end1, end2,
-    b0, b1, b2, rb0, rb1, rb2, c0, c1, c2, rc0, rc1, rc2, wg_ref, twin_wg_ref,
-    load_sem, table_sem, gs, g1r, g2r, g3r, gfr, gcr, ts, tr, es, er, rs, par, per, br, cr,
+    b0, b1, b2, bp0, bp1, bp2, rb0, rb1, rb2, c0, c1, c2, rc0, rc1, rc2, wg_ref, twin_wg_ref,
+    load_sem, table_sem, gs, g1r, g2r, g3r, gfr, gcr, ts, tr, es, er, rs, par, per, bpr, br, cr,
 ):
     parts = range(3)
     terms, own = (t0, t1, t2), (own0, own1, own2)
     pass_up, pass_down = (pass_up0, pass_up1, pass_up2), (pass_down0, pass_down1, pass_down2)
     end = (end0, end1, end2)
-    mid, mid_in = (b0, b1, b2), (rb0, rb1, rb2)
+    mid, mid_pass, mid_in = (b0, b1, b2), (bp0, bp1, bp2), (rb0, rb1, rb2)
     last, last_in = (c0, c1, c2), (rc0, rc1, rc2)
 
     me = lax.axis_index("dev")
@@ -321,14 +321,15 @@
             value = jnp.concatenate(halves, axis=0)
             if extras:
                 value = value.astype(F32)
-                for extra in extras:
-                    value = value + extra[fast].astype(F32)
+                for extra, first in extras:
+                    if 0 <= fast - first < extra.shape[0]:
+                        value = value + extra[fast - first].astype(F32)
                 value = value.astype(BF16)
             values.append(value)
         for fast in range(SIDE):
             dst[fast] = values[fast]
 
-    away = (2, 1, 3, 0)
+    away = (2, 1, 0, 3)
 
     def middle_at(p, q):
         return (at[ORDER[p][1]] + away[q]) % SIDE
@@ -341,40 +342,63 @@
 
     up = [device(ORDER[p][0], 1) for p in parts]
     down = [device(ORDER[p][0], 3) for p in parts]
-    for q in (0, 2, 1, 3):
-        for p in parts:
-            ref = own_slab(p, 2, q)
-            if q < 2:
-                send(ref, pass_up[p].at[q], rs.at[p], par.at[p, q], up[p])
-            else:
-                send(ref, pass_down[p].at[q - 2], rs.at[p], par.at[p, q], down[p])
-    for q in range(2):
-        for p in parts:
-            send(own_slab(p, 1, q + 2), end[p].at[q + 2, 0], rs.at[p], per.at[p, q + 2], up[p])
+    def start_pass(p, q):
+        ref = own_slab(p, 2, q)
+        if q < 2:
+            send(ref, pass_up[p].at[q], rs.at[p], par.at[p, q], up[p])
+        else:
+            send(ref, pass_down[p].at[q - 2], rs.at[p], par.at[p, q], down[p])
+
+    def plain_end(p, q):
+        if q < 2:
             send(own_slab(p, 3, q), end[p].at[q, 1], rs.at[p], per.at[p, q], down[p])
-    for q in range(2):
-        for p in parts:
+        else:
+            send(own_slab(p, 1, q), end[p].at[q, 0], rs.at[p], per.at[p, q], up[p])
+
+    def passed_end(p, q):
+        if q < 2:
             arrived(pass_up[p].at[q], par.at[p, q])
-            ref = own_slab(p, 1, q, (pass_up[p].at[q],))
+            ref = own_slab(p, 1, q, ((pass_up[p].at[q], 0),))
             send(ref, end[p].at[q, 0], rs.at[p], per.at[p, q], up[p])
-            arrived(pass_down[p].at[q], par.at[p, 2 + q])
-            ref = own_slab(p, 3, q + 2, (pass_down[p].at[q],))
-            send(ref, end[p].at[q + 2, 1], rs.at[p], per.at[p, q + 2], down[p])
-    for q in range(4):
-        for p in parts:
-            arrived(end[p].at[q], per.at[p, q])
-            spread(p, at[ORDER[p][0]], middle_at(p, q), mid[p].at[q], (end[p].at[q, 0], end[p].at[q, 1]))
-            if q < 3:
-                send(mid[p].at[q], mid_in[p].at[q], rs.at[p], br.at[p], device(ORDER[p][1], away[q]))
+        else:
+            arrived(pass_down[p].at[q - 2], par.at[p, q])
+            ref = own_slab(p, 3, q, ((pass_down[p].at[q - 2], 0),))
+            send(ref, end[p].at[q, 1], rs.at[p], per.at[p, q], down[p])
+
+    def finish_slab(p, q):
+        arrived(end[p].at[q], per.at[p, q])
+        extras = [(end[p].at[q, 0], 0), (end[p].at[q, 1], 0)]
+        above, below = device(ORDER[p][1], 1), device(ORDER[p][1], 3)
+        if q == 1:
+            arrived(mid_pass[p].at[0], bpr.at[p, 0])
+            extras.append((mid_pass[p].at[0], 0))
+        if q == 3:
+            arrived(mid_pass[p].at[1], bpr.at[p, 1])
+            extras.append((mid_pass[p].at[1], 2))
+        spread(p, at[ORDER[p][0]], middle_at(p, q), mid[p].at[q], extras)
+        if q == 0:
+            send(mid[p].at[q, pl.ds(0, 2)], mid_pass[p].at[0], rs.at[p], bpr.at[p, 0], above)
+            send(mid[p].at[q, pl.ds(2, 2)], mid_pass[p].at[1], rs.at[p], bpr.at[p, 1], below)
+        if q == 1:
+            send(mid[p].at[q], mid_in[p].at[0], rs.at[p], br.at[p], above)
+        if q == 3:
+            send(mid[p].at[q], mid_in[p].at[1], rs.at[p], br.at[p], below)
+
+    early, late = (0, 2), (1, 3)
+    for what, slabs in (
+        (start_pass, early), (plain_end, early), (start_pass, late), (passed_end, early),
+        (plain_end, late), (passed_end, late), (finish_slab, early), (finish_slab, late),
+    ):
+        for q in slabs:
+            for p in parts:
+                what(p, q)
     for p in parts:
         arrived(mid_in[p], br.at[p])
-        total = mid[p][3].astype(F32)
-        for q in range(3):
-            total = total + mid_in[p][q].astype(F32)
+        total = mid[p][2].astype(F32) + mid_in[p][0].astype(F32) + mid_in[p][1].astype(F32)
         last[p][...] = total.astype(BF16)
-        for q in range(3):
-            place = (at[ORDER[p][2]] + away[q]) % SIDE
-            send(last[p].at[place], last_in[p].at[q], rs.at[p], cr.at[p], device(ORDER[p][2], away[q]))
+        for q, hop in enumerate((2, 1, 3)):
+            place = (at[ORDER[p][2]] + hop) % SIDE
+            send(last[p].at[place], last_in[p].at[q], rs.at[p], cr.at[p], device(ORDER[p][2], hop))
     results = []
     for p in parts:
         arrived(last_in[p], cr.at[p])
@@ -403,8 +427,8 @@
     weight_grad_ref[...] = weight_grad_in[...]
 
 
-FORWARD_UNROLL = 4
-TERM_UNROLL = 4
+FORWARD_UNROLL = 8
+TERM_UNROLL = 8
 
 
 def on_device(features, weight, tile_values, tile_cols, tile_counts, cotangent):
@@ -429,12 +453,13 @@
         + three(2, 4, rows=CHUNK)
         + three(4, 2, 4, rows=CHUNK)
         + three(4, 4, rows=CHUNK)
-        + three(3, 4, rows=CHUNK)
+        + three(2, 2, rows=CHUNK)
+        + three(2, 4, rows=CHUNK)
         + three(4, rows=CHUNK)
         + three(3, rows=CHUNK)
         + [vmem(2 * FIN, TILE, dtype=F32)] * 2
         + [dma((8,)), dma((3,)), dma((3,)), dma((3, 3)), dma((3, 12)), dma((3, 8)), dma((3, 4)), dma((3,))]
-        + [dma((3,)), dma((3,)), dma((2,)), dma((2,)), dma((3,)), dma((3, 4)), dma((3, 4)), dma((3,)), dma((3,))]
+        + [dma((3,)), dma((3,)), dma((2,)), dma((2,)), dma((3,)), dma((3, 4)), dma((3, 4)), dma((3, 2)), dma((3,)), dma((3,))]
     )
     shapes = (
         jax.ShapeDtypeStruct((256, HID), BF16),

time: 63.7 us -> 62 us (0.973)
  Pallas kernels: 62.9 us -> 61.3 us
    pallas_call x1, Pallas kernels: 62.2 us -> 60.6 us  [on_device(): pl.pallas_call(kernel, out_shape=shapes, in_specs=[in_hbm] * 6, out_specs...]
where the time goes in v5:
time: 62 us; the launch traced here: 61.9 us
  Pallas kernels  61.3 us (99%)
  between operations  0.64 us (1%)
    pallas_call x1, Pallas kernels, on_device(): pl.pallas_call(kernel, out_shape=shapes, in_specs=[in_hbm] * 6, out_specs...  60.6 us

profile of v5, /device:TPU:0, one launch (start us, length us, event | category | flops | bytes accessed | tf_op | source)
XLA Modules:
  0.0 61.9 jit_solution(2499957582629541737)
XLA Ops:
  0.6 60.6 %graph_layer.1 = (bf16[256,256]{1,0:T(8,128)(2,1)S(1)}, f32[256,128]{1,0:T(8,128)S(1)}, f32[1,256]{1,0:T(1,128)S(1)}) custom-call(bf16[16,16,128]{2,1,0:T(8,128)(2,1)} %bitcast.1, bf16[128,256]{1,0:T(8,128)(2,1)} %weight_hbm.1, bf16[2,32,128,128]{3,2,1,0:T(8,128)(2,1)} %tiles_hbm.1, s32[2,32]{1,0:T(2,128)} %cols_hbm.1, s32[2,32]{1,0:T(2,128)} %counts_hbm.1, ...), custom_call_target="tpu_custom_call" | custom-call | tf_op jit(solution)/shard_map/graph_layer/pallas_call | solution.py:469
  61.2 0.7 %hand_over.1 = (bf16[256,256]{1,0:T(8,128)(2,1)}, f32[256,128]{1,0:T(8,128)}, f32[1,256]{1,0:T(1,128)}) custom-call(bf16[256,256]{1,0:T(8,128)(2,1)S(1)} %get-tuple-element.6.act_in, f32[256,128]{1,0:T(8,128)S(1)} %get-tuple-element.7.grad_in, f32[1,256]{1,0:T(1,128)S(1)} %get-tuple-element.8.weight_grad_in), custom_call_target="tpu_custom_call" | custom-call | tf_op jit(solution)/shard_map/hand_over/pallas_call | solution.py:483

commit v6 on v5

--- a/solution.py
+++ b/solution.py
@@ -119,7 +119,7 @@
         if r > 0:
             arrived(ref, g1r.at[p, r - 1])
         for n, hop in enumerate(HOPS):
-            send(ref, ref, gs.at[p], g2r.at[p, r * 3 + n], move(i2[p], s2[p], hop))
+            send(ref, ref, gs.at[p], g2r.at[p, r], move(i2[p], s2[p], hop))
         return ref
 
     for p in parts:
@@ -138,10 +138,9 @@
         send(ref, ref, gs.at[p], gcr.at[p], twin)
 
     def last_sends(p, r):
-        for n, hop in enumerate(HOPS):
-            ref = chunk(p, i3[p], fast_at(p, r), (i2[p] + SIDE - hop) % SIDE)
-            arrived(ref, g2r.at[p, r * 3 + n])
-            along_third(p, r, ref)
+        arrived(group(p, i3[p], r, 0, 3), g2r.at[p, r])
+        for hop in HOPS:
+            along_third(p, r, chunk(p, i3[p], fast_at(p, r), (i2[p] + SIDE - hop) % SIDE))
         to_the_twin(p, group(p, i3[p], r))
 
     def pass_on(p, r):
@@ -264,12 +263,19 @@
         weight, delta, (((1,), (1,)), ((), ())), preferred_element_type=F32
     ).astype(BF16)
 
+    weight_terms = lax.dot_general(
+        aggregated, delta, (((0,), (0,)), ((), ())), preferred_element_type=F32
+    )
+    for which in range(2):
+        wg_ref[pl.ds(which * FIN, FIN), :] = weight_terms[:, which * TILE : (which + 1) * TILE]
+    send(wg_ref, twin_wg_ref, es.at[1], er.at[1], twin)
+
     for b in range(2):
         left_factor = back[:, b * TILE : (b + 1) * TILE]
-        for group in range(2):
+        for group in range(4):
             def term_step(n, carry, b=b, group=group, left_factor=left_factor):
                 for k in range(TERM_UNROLL):
-                    slot = group * 16 + (n * TERM_UNROLL + k) * 2
+                    slot = group * 8 + (n * TERM_UNROLL + k) * 2
                     right = jnp.concatenate([tiles[b, slot], tiles[b, slot + 1]], axis=1)
                     both = jnp.dot(left_factor, right, preferred_element_type=F32).astype(BF16)
                     for which in range(2):
@@ -279,19 +285,13 @@
                             ]
                 return carry
 
-            lax.fori_loop(0, 8 // TERM_UNROLL, term_step, 0)
+            lax.fori_loop(0, 4 // TERM_UNROLL, term_step, 0)
             for p in parts:
-                first = b * SLOTS + group * 16
+                first = b * SLOTS + group * 8
                 send(
-                    terms[p].at[pl.ds(first, 16)], terms[p].at[pl.ds(2 * SLOTS + first, 16)],
+                    terms[p].at[pl.ds(first, 8)], terms[p].at[pl.ds(2 * SLOTS + first, 8)],
                     ts.at[p], tr.at[p], twin,
                 )
-    weight_terms = lax.dot_general(
-        aggregated, delta, (((0,), (0,)), ((), ())), preferred_element_type=F32
-    )
-    for which in range(2):
-        wg_ref[pl.ds(which * FIN, FIN), :] = weight_terms[:, which * TILE : (which + 1) * TILE]
-    send(wg_ref, twin_wg_ref, es.at[1], er.at[1], twin)
     twin_slot_copy.wait()
     for p in parts:
         arrived(terms[p].at[pl.ds(2 * SLOTS, 2 * SLOTS)], tr.at[p])
@@ -428,7 +428,7 @@
 
 
 FORWARD_UNROLL = 8
-TERM_UNROLL = 8
+TERM_UNROLL = 4
 
 
 def on_device(features, weight, tile_values, tile_cols, tile_counts, cotangent):
@@ -458,7 +458,7 @@
         + three(4, rows=CHUNK)
         + three(3, rows=CHUNK)
         + [vmem(2 * FIN, TILE, dtype=F32)] * 2
-        + [dma((8,)), dma((3,)), dma((3,)), dma((3, 3)), dma((3, 12)), dma((3, 8)), dma((3, 4)), dma((3,))]
+        + [dma((8,)), dma((3,)), dma((3,)), dma((3, 3)), dma((3, 4)), dma((3, 8)), dma((3, 4)), dma((3,))]
         + [dma((3,)), dma((3,)), dma((2,)), dma((2,)), dma((3,)), dma((3, 4)), dma((3, 4)), dma((3, 2)), dma((3,)), dma((3,))]
     )
     shapes = (

time: 62 us -> 61.6 us (level)
  no operation moved by 1% of the time
where the time goes in v6:
time: 61.6 us; the launch traced here: 61.5 us
  Pallas kernels  60.8 us (99%)
  between operations  0.64 us (1%)
    pallas_call x1, Pallas kernels, on_device(): pl.pallas_call(kernel, out_shape=shapes, in_specs=[in_hbm] * 6, out_specs...  60.1 us

profile of v6, /device:TPU:0, one launch (start us, length us, event | category | flops | bytes accessed | tf_op | source)
XLA Modules:
  0.0 61.5 jit_solution(3540884399976193094)
XLA Ops:
  0.6 60.1 %graph_layer.1 = (bf16[256,256]{1,0:T(8,128)(2,1)S(1)}, f32[256,128]{1,0:T(8,128)S(1)}, f32[1,256]{1,0:T(1,128)S(1)}) custom-call(bf16[16,16,128]{2,1,0:T(8,128)(2,1)} %bitcast.1, bf16[128,256]{1,0:T(8,128)(2,1)} %weight_hbm.1, bf16[2,32,128,128]{3,2,1,0:T(8,128)(2,1)} %tiles_hbm.1, s32[2,32]{1,0:T(2,128)} %cols_hbm.1, s32[2,32]{1,0:T(2,128)} %counts_hbm.1, ...), custom_call_target="tpu_custom_call" | custom-call | tf_op jit(solution)/shard_map/graph_layer/pallas_call | solution.py:469
  60.8 0.7 %hand_over.1 = (bf16[256,256]{1,0:T(8,128)(2,1)}, f32[256,128]{1,0:T(8,128)}, f32[1,256]{1,0:T(1,128)}) custom-call(bf16[256,256]{1,0:T(8,128)(2,1)S(1)} %get-tuple-element.6.act_in, f32[256,128]{1,0:T(8,128)S(1)} %get-tuple-element.7.grad_in, f32[1,256]{1,0:T(1,128)S(1)} %get-tuple-element.8.weight_grad_in), custom_call_target="tpu_custom_call" | custom-call | tf_op jit(solution)/shard_map/hand_over/pallas_call | solution.py:483
